TPU v7x, 32 devices: a whole 2x2x4 slice. The times are simulated.
32 devices in a mesh: expert: 32 (over z, y, x, core), mp: 1.
Axes of the slice: x: 2, y: 2, z: 4, core: 2. Of those that a mesh axis runs over, the one named last changes fastest.
Arguments:
- hidden_state: bfloat16 [4096, 2048], P('expert', 'mp'), as said below
- context: bfloat16 [4096, 2048], P('expert', 'mp'), may hold values from -6 to 6
- out_proj: bfloat16 [2048, 2048], P('mp', 'expert'), may hold values from -0.125 to 0.125
- norm_gain: bfloat16 [2048], P('mp'), may hold values from 0.25 to 1.75
- router_weight: float32 [2048, 32], P('mp'), as said below
- expert_in: bfloat16 [32, 2048, 2, 1408], P('expert', None, None, 'mp'), may hold values from -0.125 to 0.125
- expert_out: bfloat16 [32, 1408, 2048], P('expert', 'mp'), may hold values from -0.15625 to 0.15625
- shared_in: bfloat16 [2048, 2, 2816], P('expert', None, 'mp'), may hold values from -0.125 to 0.125
- shared_out: bfloat16 [2816, 2048], P('mp', 'expert'), may hold values from -0.109375 to 0.109375
- route_ids: int32 [4096, 6], P('expert'), may hold values from 0 to 31, all different within a row; in each aligned block of 128 rows (0 to 127, 128 to 255, ...) at most 40 rows name the same one
Outputs:
- output: float32 [4096, 2048], P('expert', 'mp')
Inputs may be any that keep to these rules, and one draw needn't show every extreme that they name: `route_ids`: each row names 6 different experts; among the rows of one index of the expert axis no expert is named by more than 40 rows. `router_weight`: finite float32 router columns; no range is promised. `hidden_state`: finite values; no range is promised.
All inputs are finite; a program needn't handle non-finite values.
Results may differ from a plain program's by a relative error of at most 0.0025.
Values may be sent and summed in bfloat16 or wider, within the bound.
No kernel may reach another device: no remote copies, remote signals or barrier semaphores. Data moves between devices by JAX's collectives and lax.ppermute only.
A program may use at most 128 MiB of HBM per device.

v0:
```python
import functools

import jax
import jax.numpy as jnp
from jax import lax
from jax.experimental import pallas as pl
from jax.experimental.pallas import tpu as pltpu
from jax.sharding import PartitionSpec as P

LANES = 128
LAYER = 8


def capacity_of(rows, top, experts):
    return max(2, min(rows, rows * top // experts * 5 // 3))


def general(
    hidden_state,
    context,
    out_proj,
    norm_gain,
    router_weight,
    expert_in,
    expert_out,
    shared_in,
    shared_out,
    route_ids,
):
    rows_here, top = route_ids.shape
    experts = router_weight.shape[1]
    width = out_proj.shape[0] * lax.axis_size("mp")
    capacity = capacity_of(rows_here, top, experts)
    partial_attn = jnp.dot(
        context,
        lax.all_gather(out_proj, "expert", axis=1, tiled=True),
        preferred_element_type=jnp.float32,
    )
    attn = lax.psum_scatter(partial_attn, "mp", scatter_dimension=1, tiled=True)
    mixed = hidden_state.astype(jnp.float32) + attn
    gain = norm_gain.astype(jnp.float32)
    squares = lax.psum(jnp.sum(mixed * mixed, axis=1), "mp")
    inverse = lax.rsqrt(squares / width + 1e-06)[:, None]
    normed32 = mixed * inverse * gain
    logits = lax.psum(jnp.dot(normed32, router_weight, precision=lax.Precision.HIGHEST), "mp")
    normed = normed32.astype(jnp.bfloat16)
    gates = jax.nn.softmax(jnp.take_along_axis(logits, route_ids, axis=1), axis=1)
    full_rows = lax.all_gather(normed, "mp", axis=1, tiled=True)
    shared_width = shared_in.shape[2]
    piece = lax.all_gather(shared_in, "expert", axis=0, tiled=True)
    shared_both = jnp.dot(
        full_rows,
        piece.reshape(piece.shape[0], 2 * shared_width),
        preferred_element_type=jnp.float32,
    )
    shared_both = shared_both.reshape(rows_here, 2, shared_width)
    shared_hidden = (jax.nn.silu(shared_both[:, 0]) * shared_both[:, 1]).astype(jnp.bfloat16)
    shared_part = jnp.dot(
        shared_hidden,
        lax.all_gather(shared_out, "expert", axis=1, tiled=True),
        preferred_element_type=jnp.float32,
    )
    flat = route_ids.reshape(-1)
    onehot = (flat[:, None] == jnp.arange(experts, dtype=jnp.int32)[None, :]).astype(jnp.int32)
    position = jnp.sum(onehot * jnp.cumsum(onehot, axis=0), axis=1) - 1
    slot_of = flat * capacity + position
    source = (
        jnp.zeros((experts * capacity,), jnp.int32)
        .at[slot_of]
        .set(jnp.arange(flat.shape[0], dtype=jnp.int32) // top)
    )
    filled = jnp.zeros((experts * capacity,), jnp.bool_).at[slot_of].set(True)
    outgoing = jnp.where(filled[:, None], normed[source], jnp.zeros((), jnp.bfloat16)).reshape(
        experts, capacity, normed.shape[1]
    )
    quarter = expert_in.shape[3]
    weights_in = expert_in[0].reshape(width, 2 * quarter)
    incoming = lax.all_to_all(outgoing, "expert", split_axis=0, concat_axis=0, tiled=True)
    sources = incoming.shape[0]
    items = incoming.shape[1]
    gathered = lax.all_gather(incoming, "mp", axis=2, tiled=True).reshape(sources * items, width)
    inner = jnp.dot(gathered, weights_in, preferred_element_type=jnp.float32).reshape(
        -1, 2, quarter
    )
    hidden = (jax.nn.silu(inner[:, 0]) * inner[:, 1]).astype(jnp.bfloat16)
    partial_out = jnp.dot(hidden, expert_out[0], preferred_element_type=jnp.float32).astype(
        jnp.bfloat16
    )
    partial_out = partial_out.reshape(sources, items, width)
    result = lax.all_to_all(partial_out, "expert", split_axis=0, concat_axis=0, tiled=True)
    picked = result.reshape(experts * capacity, result.shape[2])[slot_of]
    slot_total = lax.psum_scatter(
        lax.optimization_barrier(picked).astype(jnp.float32).astype(jnp.bfloat16),
        "mp",
        scatter_dimension=1,
        tiled=True,
    )
    expert_sum = lax.optimization_barrier(slot_total).astype(jnp.float32)
    expert_sum = expert_sum.reshape(rows_here, top, expert_sum.shape[1])
    routed = jnp.sum(gates[:, :, None] * expert_sum, axis=1)
    shared = lax.psum_scatter(shared_part, "mp", scatter_dimension=1, tiled=True)
    return mixed + routed + shared


def swap(x, bit):
    n = lax.axis_size("expert")
    return lax.ppermute(x, "expert", [(i, i ^ bit) for i in range(n)])


def silu(v):
    return v / (1.0 + jnp.exp(-v))


def spread_first(block, rows):
    half = block.shape[1] // 2
    h0, h1 = block[:, :half], block[:rows, half:]
    return jnp.concatenate([h0, swap(h0, 2)], axis=0), jnp.concatenate([h1, swap(h1, 4)], axis=0)


def spread_second(l0, l1):
    return l0, swap(l0, 4), l1, swap(l1, 2)


def along_z(block, layers):
    blocks = [block]
    for k in range(1, layers):
        low = k & -k
        blocks.append(swap(blocks[k - low], LAYER * low))
    return blocks


def tie(x, *others):
    return lax.optimization_barrier((x, *others))[0]


class Copies:
    def __init__(self, sems):
        self.sems, self.all = sems, []

    def start(self, src, dst):
        c = pltpu.make_async_copy(src, dst, self.sems.at[len(self.all)])
        c.start()
        self.all.append(c)

    def wait(self):
        for c in self.all:
            c.wait()


PIECES = ((0, 0, (0, 1)), (1, 0, (2, 3)), (2, 1, (0, 2)), (3, 1, (1, 3)))


def fetch_rows(copies, pieces, rows, xs):
    half = xs.shape[1] // 2
    for n, h, chips in PIECES:
        stride = pieces[n].shape[0] // 2
        for a, q in enumerate(chips):
            copies.start(
                pieces[n].at[pl.ds(a * stride, rows)],
                xs.at[pl.ds(q * rows, rows), pl.ds(h * half, half)],
            )


def fetch_gates(copies, left, rows, to):
    for piece, (_, _, chips) in zip(left, PIECES):
        stride = piece.shape[0] // 2
        for a, q in enumerate(chips):
            copies.start(piece.at[pl.ds(a * stride + rows, stride - rows)], to.at[q])


def slots_of(sent, idx_ref, expert, experts, cap, rows):
    extra, half = sent.shape[1:]
    each = half // rows
    tall = experts // each
    line, column = idx_ref[2 * expert], idx_ref[2 * expert + 1]
    r = lax.broadcasted_iota(jnp.int32, (extra, half), 0)
    wanted = (r == line) | (r == line + tall) | (r == line + 2 * tall)
    found = []
    for q in range(4):
        parts = jnp.where(wanted, sent[q].astype(jnp.float32), 0.0)
        parts = jnp.sum(parts, axis=0, keepdims=True)
        g = jnp.zeros((1, rows), jnp.float32)
        for j in range(each):
            g = jnp.where(column == j, parts[:, j * rows : (j + 1) * rows], g)
        found.append(g)
    g = jnp.concatenate(found, axis=0)
    chosen = g > 0.0
    r_io = lax.broadcasted_iota(jnp.int32, (rows, rows), 0)
    c_io = lax.broadcasted_iota(jnp.int32, (rows, rows), 1)
    upto = jnp.where(r_io <= c_io, 1.0, 0.0).astype(jnp.bfloat16)
    count = jnp.dot(
        jnp.where(chosen, 1.0, 0.0).astype(jnp.bfloat16), upto, preferred_element_type=jnp.float32
    ).astype(jnp.int32)
    first = lax.broadcasted_iota(jnp.int32, (4, rows), 0) * cap
    return g, jnp.where(chosen, first + count - 1, -1)


def steps(total, most):
    step = min(most, total)
    return [(n, step) for n in range(0, total, step)]


def attention_kernel(groups, rows, idx_ref, mine_ref, other_ref, *rest):
    pieces, (keep_ref, send_ref, w_v, sems) = rest[: 4 * groups], rest[4 * groups :]
    half = w_v.shape[1] // 2
    count = pieces[0].shape[0] // (2 * rows)
    copies = Copies(sems)
    for g in range(groups):
        l0, r0, l1, r1 = pieces[4 * g : 4 * g + 4]
        for h, (near, far, first, second) in enumerate(((l0, r0, 1, 2), (l1, r1, 2, 1))):
            for piece, base in ((near, 0), (far, second)):
                for a, q in enumerate((base, base + first)):
                    for i in range(count):
                        chip = idx_ref[(g * count + i) * 4 + q]
                        to = pl.ds(pl.multiple_of(chip * rows, rows), rows)
                        copies.start(
                            piece.at[pl.ds((a * count + i) * rows, rows)],
                            w_v.at[to, pl.ds(h * half, half)],
                        )
    copies.wait()
    both = jnp.concatenate([mine_ref[...], other_ref[...]], axis=0)
    here = mine_ref.shape[0]
    for n, step in steps(w_v.shape[0], 512):
        part = lax.dot_general(
            both,
            w_v[pl.ds(n, step), :],
            (((1,), (1,)), ((), ())),
            preferred_element_type=jnp.float32,
        )
        keep_ref[:, pl.ds(n, step)] = part[:here]
        send_ref[:, pl.ds(n, step)] = part[here:]


def pick_kernel(cap, rows, experts, unused, idx_ref, *rest):
    pieces = rest[:4]
    mine_ref, other_ref, xs, sent, pick, out_v, x_sem, g_sem, o_sem = rest[4 + unused :]
    gates, copies = Copies(g_sem), Copies(x_sem)
    fetch_gates(gates, pieces[:2], rows, sent)
    fetch_rows(copies, pieces, rows, xs)
    slots = 4 * cap
    numbers = lax.broadcasted_iota(jnp.int32, (slots, rows), 0)
    gates.wait()
    for e in range(2):
        _, slot = slots_of(sent, idx_ref, e, experts, cap, rows)
        for q in range(4):
            pick[pl.ds(e * slots, slots), pl.ds(q * rows, rows)] = jnp.where(
                numbers == slot[q : q + 1, :], 1.0, 0.0
            ).astype(jnp.bfloat16)
    copies.wait()
    for n, step in steps(xs.shape[1], 512):
        out_v[:, pl.ds(n, step)] = jnp.dot(
            pick[...], xs[:, pl.ds(n, step)], preferred_element_type=jnp.float32
        ).astype(jnp.bfloat16)
    outs = Copies(o_sem)
    outs.start(out_v.at[pl.ds(slots, slots)], other_ref)
    outs.start(out_v.at[pl.ds(0, slots)], mine_ref)
    outs.wait()


def shared_kernel(rows, unused, three_ref, theirs_ref, *rest):
    pieces, (hs_ref, xs, w_v, x_sem) = rest[:4], rest[4 + unused :]
    hp = three_ref.shape[3]
    copies = Copies(x_sem)
    fetch_rows(copies, pieces, rows, xs)
    for e, ref in enumerate((three_ref, theirs_ref)):
        for h in range(2):
            copies.start(ref.at[:, h], w_v.at[:, :, pl.ds((2 * h + e) * hp, hp)])
    copies.wait()
    w = w_v[...].reshape(xs.shape[1], 4 * hp)
    for m, step in steps(4 * rows, 2 * rows):
        both = jnp.dot(xs[pl.ds(m, step), :], w, preferred_element_type=jnp.float32)
        hs_ref[pl.ds(m, step), :] = (silu(both[:, : 2 * hp]) * both[:, 2 * hp :]).astype(
            jnp.bfloat16
        )


def expert_kernel(unused, mine_ref, other_ref, win_ref, wout_ref, *rest):
    mine_out, other_out, x_v, win_v, wout_v, hid_v, y_v, x_sem, w_sem, o_sem = rest[unused:]
    slots, wide = mine_ref.shape
    tiles, tile = win_v.shape[0], win_v.shape[3] // 2
    rows = Copies(x_sem)
    rows.start(mine_ref, x_v.at[pl.ds(0, slots)])
    rows.start(other_ref, x_v.at[pl.ds(slots, slots)])
    copies = Copies(w_sem)
    for t in range(tiles):
        for h in range(2):
            copies.start(
                win_ref.at[:, h, :, pl.ds(t * tile, tile)],
                win_v.at[t, :, :, pl.ds(h * tile, tile)],
            )
    copies.start(wout_ref, wout_v)
    rows.wait()
    here = 0
    for t in range(tiles):
        if t == here:
            here = min(2 * here + 1, tiles)
            for c in copies.all[2 * t : 2 * here]:
                c.wait()
        both = jnp.dot(
            x_v[...], win_v[t].reshape(wide, 2 * tile), preferred_element_type=jnp.float32
        )
        hid_v[:, pl.ds(t * tile, tile)] = (silu(both[:, :tile]) * both[:, tile:]).astype(
            jnp.bfloat16
        )
    copies.all[2 * tiles].wait()
    outs = Copies(o_sem)
    for n, step in steps(wide, 512):
        y_v[:, pl.ds(n, step)] = jnp.dot(
            hid_v[...], wout_v[:, pl.ds(n, step)], preferred_element_type=jnp.float32
        ).astype(jnp.bfloat16)
    outs.start(y_v.at[pl.ds(slots, slots)], other_out)
    outs.start(y_v.at[pl.ds(0, slots)], mine_out)
    outs.wait()


def place_kernel(cap, rows, experts, unused, idx_ref, mine_ref, other_ref, hs_ref, *rest):
    three_ref, theirs_ref, l0, r0 = rest[:4]
    refs, rest = rest[4 + unused : 8 + unused], rest[8 + unused :]
    bufs, (w_v, sent, place, gate_col, g_sem, w_sem, o_sem) = rest[:4], rest[4:]
    near_low, far_low, near_high, far_high = bufs
    wide, half = mine_ref.shape[1], near_low.shape[1]
    hp = three_ref.shape[3]
    slots = 4 * cap
    f32 = jnp.float32
    gates, copies = Copies(g_sem), Copies(w_sem)
    fetch_gates(gates, (l0, r0), rows, sent)
    for e, ref in enumerate((three_ref, theirs_ref)):
        copies.start(ref.at[:, 2], w_v.at[:, :, pl.ds(e * hp, hp)])
    r_io = lax.broadcasted_iota(jnp.int32, (rows, rows), 0)
    c_io = lax.broadcasted_iota(jnp.int32, (rows, rows), 1)
    eye = r_io == c_io
    numbers = lax.broadcasted_iota(jnp.int32, (rows, slots), 1)
    gates.wait()
    for e in range(2):
        g, slot = slots_of(sent, idx_ref, e, experts, cap, rows)
        for q in range(4):
            at = pl.ds(q * rows, rows)
            col = jnp.sum(jnp.where(eye, slot[q : q + 1, :], 0), axis=1, keepdims=True)
            place[e, at, :] = jnp.where(numbers == col, 1.0, 0.0).astype(jnp.bfloat16)
            gcol = jnp.sum(jnp.where(eye, g[q : q + 1, :], 0.0), axis=1, keepdims=True)
            gate_col[e, at, :] = jnp.broadcast_to(gcol, (rows, LANES))
    copies.wait()
    depth = w_v.shape[1]
    outs = Copies(o_sem)
    for n, step in steps(wide, min(256, half)):
        cols = pl.ds(n, step)
        if step % depth == 0:
            down = w_v[pl.ds(n // depth, step // depth)].reshape(step, 2 * hp)
        else:
            down = w_v[...].reshape(wide, 2 * hp)[n : n + step]
        total = lax.dot_general(
            hs_ref[...], down, (((1,), (1,)), ((), ())), preferred_element_type=f32
        )
        for e, ref in enumerate((mine_ref, other_ref)):
            y = jnp.dot(place[e], ref[:, cols], preferred_element_type=f32)
            total = total + gate_col[e][:, 0:1] * y
        if n < half:
            near, far, order, at = near_low, far_low, (0, 1, 2, 3), pl.ds(n, step)
        else:
            near, far, order, at = near_high, far_high, (0, 2, 1, 3), pl.ds(n - half, step)
        for a in range(2):
            to = pl.ds(a * rows, rows)
            q = order[a] * rows
            near[to, at] = total[q : q + rows]
            q = order[2 + a] * rows
            far[to, at] = total[q : q + rows].astype(far.dtype)
        if (n + step) % half == 0:
            k = 2 * (n // half)
            outs.start(bufs[k + 1], refs[k + 1])
            outs.start(bufs[k], refs[k])
    outs.wait()


def call(body, out_shape, in_specs, args, scratch, after=(), outs_in_vmem=True):
    vmem = pl.BlockSpec(memory_space=pltpu.VMEM)
    hbm = pl.BlockSpec(memory_space=pl.ANY)
    kinds = {"s": pl.BlockSpec(memory_space=pltpu.SMEM), "v": vmem, "h": hbm}
    return pl.pallas_call(
        body,
        out_shape=out_shape,
        in_specs=[kinds[k] for k in in_specs] + [hbm] * len(after),
        out_specs=tuple([vmem if outs_in_vmem else hbm] * len(out_shape)),
        scratch_shapes=scratch,
        compiler_params=pltpu.CompilerParams(vmem_limit_bytes=48 * 1024 * 1024),
        cost_estimate=pl.CostEstimate(flops=1, bytes_accessed=1, transcendentals=0),
    )(*args, *after)


def attention(context, out_proj, before, exchange):
    bf, f32 = jnp.bfloat16, jnp.float32
    me = lax.axis_index("expert")
    layers = lax.axis_size("expert") // LAYER
    odd = me % 2 == 1
    wide = context.shape[1]
    half = wide // 2

    def halves(lo, hi):
        return jnp.where(odd, hi, lo), jnp.where(odd, lo, hi)

    turned = out_proj.T
    mine, other = halves(turned[:, :half], turned[:, half:])
    pair = jnp.concatenate(halves(mine, swap(other, 1)), axis=0)
    mine, other = halves(context[:, :half], context[:, half:])
    got = swap(other, 1)
    cut = pair.shape[0]
    blocks = along_z(pair, layers)
    twos = [list(range(i, min(i + 2, layers))) for i in range(0, layers, 2)]
    firsts = [
        spread_first(jnp.concatenate([blocks[k] for k in two], axis=0), cut * len(two))
        for two in twos
    ]
    exchange = lax.all_to_all(
        tie(exchange, *(v for first in firsts for v in first)),
        "expert",
        split_axis=0,
        concat_axis=0,
        tiled=True,
    )
    pieces, chips = [], []
    for two, first in zip(twos, firsts):
        pieces += spread_second(*first)
        for k in two:
            layer = jnp.bitwise_xor(me // LAYER, k)
            chips += [layer * (LAYER // 2) + jnp.bitwise_xor(me % LAYER // 2, q) for q in range(4)]
    mine, before = lax.optimization_barrier((mine, before))
    here = context.shape[0]
    keep, send = call(
        functools.partial(attention_kernel, len(twos), cut),
        [jax.ShapeDtypeStruct((here, wide), f32)] * 2,
        "svv" + "h" * len(pieces),
        (jnp.stack(chips).astype(jnp.int32), mine, got, *pieces),
        [
            pltpu.VMEM((out_proj.shape[1] * lax.axis_size("expert"), half), bf),
            pltpu.SemaphoreType.DMA((8 * layers,)),
        ],
    )
    return keep + swap(send, 1), before, exchange


def whole_rows(
    hidden_state,
    context,
    out_proj,
    norm_gain,
    router_weight,
    expert_in,
    expert_out,
    shared_in,
    shared_out,
    route_ids,
):
    bf, f32 = jnp.bfloat16, jnp.float32
    n = lax.axis_size("expert")
    layers = n // LAYER
    me = lax.axis_index("expert")
    odd = me % 2
    rows, top = route_ids.shape
    experts = router_weight.shape[1]
    wide = out_proj.shape[0]
    half = wide // 2
    cap = capacity_of(rows, top, experts)
    pack = 16
    win = expert_in[0].reshape(wide // pack, pack, 2, -1).transpose(0, 2, 1, 3)
    wout = expert_out[0]
    hidden = wout.shape[0]
    tile = LANES if hidden % LANES == 0 else hidden

    own = shared_in.shape[2] // n
    depth = shared_in.shape[0]
    hp = -(-own // LANES) * LANES
    three = jnp.concatenate([shared_in.transpose(1, 0, 2), shared_out.T[None]], axis=0)
    three = three.reshape(3, depth, n, own)
    three = jnp.pad(three, ((0, 0), (0, 0), (0, 0), (0, hp - own))).transpose(2, 0, 1, 3)

    attn, win, three = attention(context, out_proj, win, three)
    theirs = swap(three, 1)
    mixed = hidden_state.astype(f32) + attn
    inverse = lax.rsqrt(jnp.mean(mixed * mixed, axis=1, keepdims=True) + 1e-06)
    normed32 = mixed * inverse * norm_gain.astype(f32)
    normed = normed32.astype(bf)
    logits = jnp.dot(normed32, router_weight, precision=lax.Precision.HIGHEST)
    named = jnp.any(
        route_ids[:, :, None] == jnp.arange(experts, dtype=jnp.int32)[None, None, :], axis=1
    )
    highest = jnp.max(jnp.where(named, logits, -jnp.inf), axis=1, keepdims=True)
    raised = jnp.where(named, jnp.exp(logits - highest), 0.0)
    gates = raised / jnp.sum(raised, axis=1, keepdims=True)

    rest, parts = gates.T, []
    for _ in range(3):
        parts.append(lax.reduce_precision(rest, 8, 7))
        rest = rest - parts[-1]
    below = jnp.stack(parts).astype(bf).reshape(-1, half)
    extra = -(-below.shape[0] // 16) * 16
    below = jnp.pad(below, ((0, extra - below.shape[0]), (0, half)))
    blocks = along_z(jnp.concatenate([normed, below], axis=0), layers)

    each = half // rows
    chip_experts = (me, jnp.bitwise_xor(me, 1))
    idx = jnp.stack([v for e in chip_experts for v in (e // each, e % each)]).astype(jnp.int32)
    slots, span = 4 * cap, 4 * rows
    sds, dma = jax.ShapeDtypeStruct, pltpu.SemaphoreType.DMA
    xs = pltpu.VMEM((span, wide), bf)
    sent = pltpu.VMEM((4, extra, half), bf)

    def add_first(near_low, far_low, near_high, far_high):
        low = near_low + swap(far_low, 4).astype(f32)
        high = near_high + swap(far_high, 2).astype(f32)
        return low[:rows], low[rows:].astype(bf), high[:rows], high[rows:].astype(bf)

    order = [0] + sorted(range(1, layers), key=lambda k: (k != 1, -k))
    firsts, placed, once = {}, [], []

    def first(k):
        if k not in firsts:
            firsts[k] = spread_first(blocks[k], rows)
        return firsts[k]

    upcoming = spread_second(*first(0))
    for at, k in enumerate(order):
        pieces = upcoming
        after = [placed[-1][1]] if placed else [theirs]
        picked, lent = call(
            functools.partial(pick_kernel, cap, rows, experts, len(after)),
            [sds((slots, wide), bf)] * 2,
            "shhhh",
            (idx, *pieces),
            [
                xs,
                sent,
                pltpu.VMEM((2 * slots, span), bf),
                pltpu.VMEM((2 * slots, wide), bf),
                dma((8,)),
                dma((4,)),
                dma((2,)),
            ],
            after,
            False,
        )
        borrowed = swap(lent, 1)
        (hs,) = call(
            functools.partial(shared_kernel, rows, 1),
            [sds((span, 2 * hp), bf)],
            "hhhhhh",
            (three, theirs, *pieces),
            [xs, pltpu.VMEM((n, depth, 4 * hp), bf), dma((12,))],
            [lent],
        )
        after = [hs]
        if at + 1 < layers:
            after += first(order[at + 1])
        done, back = call(
            functools.partial(expert_kernel, len(after)),
            [sds((slots, wide), bf)] * 2,
            "hhhh",
            (picked, borrowed, win, wout),
            [
                pltpu.VMEM((2 * slots, wide), bf),
                pltpu.VMEM((hidden // tile, wide // pack, pack, 2 * tile), bf),
                pltpu.VMEM((hidden, wide), bf),
                pltpu.VMEM((2 * slots, hidden), bf),
                pltpu.VMEM((2 * slots, wide), bf),
                dma((2,)),
                dma((2 * (hidden // tile) + 1,)),
                dma((2,)),
            ],
            after,
            False,
        )
        after = []
        if at + 1 < layers:
            upcoming = spread_second(*first(order[at + 1]))
            back = tie(back, upcoming[1], upcoming[3])
        if placed:
            once.append(add_first(*placed[-1]))
            after = [once[-1][1], once[-1][3]]
        placed.append(
            call(
                functools.partial(place_kernel, cap, rows, experts, len(after)),
                [sds((2 * rows, half), t) for t in (f32, bf, f32, bf)],
                "svvvhhhh",
                (idx, done, swap(back, 1), hs, three, theirs, pieces[0], pieces[1]),
                [pltpu.VMEM((2 * rows, half), t) for t in (f32, bf, f32, bf)]
                + [
                    pltpu.VMEM((n, depth, 2 * hp), bf),
                    sent,
                    pltpu.VMEM((2, span, slots), bf),
                    pltpu.VMEM((2, span, LANES), f32),
                    dma((4,)),
                    dma((2,)),
                    dma((4,)),
                ],
                after,
                False,
            )
        )
    once.append(add_first(*placed[-1]))
    sums = {}
    for k, (low, far_low, high, far_high) in zip(order, once):
        low = low + swap(far_low, 2).astype(f32)
        high = high + swap(far_high, 4).astype(f32)
        sums[k] = jnp.concatenate([low, high], axis=1)
    for k in reversed(range(1, layers)):
        low = k & -k
        sums[k - low] = sums[k - low] + swap(sums[k].astype(bf), LAYER * low).astype(f32)
    return mixed + sums[0]


def solution(mesh):
    n, mp = mesh.shape["expert"], mesh.shape["mp"]
    fits = mp == 1 and n % LAYER == 0 and (n // LAYER) & (n // LAYER - 1) == 0
    per_device = whole_rows if fits else general
    return jax.shard_map(
        per_device,
        mesh=mesh,
        in_specs=(
            P("expert", "mp"),
            P("expert", "mp"),
            P("mp", "expert"),
            P("mp"),
            P("mp", None),
            P("expert", None, None, "mp"),
            P("expert", "mp", None),
            P("expert", None, "mp"),
            P("mp", "expert"),
            P("expert", None),
        ),
        out_specs=P("expert", "mp"),
        check_vma=False,
    )
```

profile of v0, /device:TPU:0, one launch (start us, length us, event | category | flops | bytes accessed | tf_op | source)
XLA Modules:
  0.0 326.2 jit_solution(2346343693941149780)
XLA Ops:
  3.6 3.0 collective-permute-start.2
  6.6 2.6 collective-permute-start.7
  10.7 2.4 reshape.19
  13.8 5.0 %collective-permute-done.2 = bf16[128,1024]{1,0:T(8,128)(2,1)} collective-permute-done((bf16[128,1024]{1,0:T(8,128)(2,1)S(1)}, bf16[128,1024]{1,0:T(8,128)(2,1)}, u32[]{:S(2)}, u32[]{:S(2)}) %collective-permute-start.2) | collective-permute-done | bytes 262176 | tf_op jit(solution)/shard_map/ppermute | solution.py:107
  24.8 2.9 collective-permute-done.8
  29.2 1.7 fusion.3
  32.6 2.0 collective-permute-done.9
  34.6 2.7 collective-permute-done.11
  38.2 4.9 %all-to-all-start = ((bf16[32,3,64,128]{3,2,1,0:T(8,128)(2,1)}), bf16[32,3,64,128]{3,2,1,0:T(8,128)(2,1)S(1)}, u32[]{:S(2)}, u32[]{:S(2)}) async-start(bf16[32,3,64,128]{3,2,1,0:T(8,128)(2,1)} %fusion.3), calls=%async_computation | async-start | bytes 3145728 | tf_op jit(solution)/shard_map/all_to_all | solution.py:412
  43.1 1.9 collective-permute-start.4
  47.2 1.9 broadcast_select_fusion
  49.1 11.3 %copy.28 = bf16[128,16,2,1408]{3,1,2,0:T(8,128)(2,1)} copy(bf16[128,16,2,1408]{3,2,1,0:T(2,128)(2,1)} %bitcast.60) | data formatting | bytes 23068672 | tf_op jit(solution)/shard_map/reshape;squeeze | solution.py:463
  60.5 11.6 %collective-permute-done.4.rest_1_ = bf16[512,512]{1,0:T(8,128)(2,1)} collective-permute-done((bf16[512,512]{1,0:T(8,128)(2,1)S(1)}, bf16[512,512]{1,0:T(8,128)(2,1)}, u32[]{:S(2)}, u32[]{:S(2)}) %collective-permute-start.4) | collective-permute-done | bytes 524320 | tf_op jit(solution)/shard_map/ppermute | solution.py:107
  72.6 12.8 %collective-permute-done.10.rest_5_ = bf16[512,512]{1,0:T(8,128)(2,1)} collective-permute-done((bf16[512,512]{1,0:T(8,128)(2,1)S(1)}, bf16[512,512]{1,0:T(8,128)(2,1)}, u32[]{:S(2)}, u32[]{:S(2)}) %collective-permute-start.10) | collective-permute-done | bytes 524320 | tf_op jit(solution)/shard_map/ppermute | solution.py:107
  87.4 5.3 %shard_map.100 = (f32[128,2048]{1,0:T(8,128)S(1)}, f32[128,2048]{1,0:T(8,128)}) custom-call(s32[16]{0:T(128)S(1)} %stack.98.idx_ref, bf16[128,1024]{1,0:T(8,128)(2,1)S(1)} %copy-done.8, bf16[128,1024]{1,0:T(8,128)(2,1)} %collective-permute-done.other_ref, bf16[512,512]{1,0:T(8,128)(2,1)S(1)} %pad_maximum_fusion.5.rest_0_, ...), custom_call_target="tpu_custom_call" | custom-call | flops 1 | bytes 1 | tf_op jit(solution)/shard_map/pallas_call | solution.py:378
  92.8 2.8 collective-permute-done.13
  98.4 1.7 fusion.9
  102.4 1.6 collective-permute-start.20
  103.9 4.6 %collective-permute-done.16 = bf16[128,1024]{1,0:T(8,128)(2,1)S(1)} collective-permute-done((bf16[128,1024]{1,0:T(8,128)(2,1)S(1)}, bf16[128,1024]{1,0:T(8,128)(2,1)S(1)}, u32[]{:S(2)}, u32[]{:S(2)}) %collective-permute-start.16) | collective-permute-done | bytes 262176 | tf_op jit(solution)/shard_map/ppermute | solution.py:107
  112.3 4.9 %collective-permute-done.20 = bf16[144,2048]{1,0:T(8,128)(2,1)S(1)} collective-permute-done((bf16[144,2048]{1,0:T(8,128)(2,1)S(1)}, bf16[144,2048]{1,0:T(8,128)(2,1)S(1)}, u32[]{:S(2)}, u32[]{:S(2)}) %collective-permute-start.20) | collective-permute-done | bytes 589856 | tf_op jit(solution)/shard_map/ppermute | solution.py:107
  120.7 3.9 %collective-permute-done.17.rest_3_ = bf16[256,1024]{1,0:T(8,128)(2,1)} collective-permute-done((bf16[256,1024]{1,0:T(8,128)(2,1)}, bf16[256,1024]{1,0:T(8,128)(2,1)}, u32[]{:S(2)}, u32[]{:S(2)}) %collective-permute-start.17) | collective-permute-done | bytes 524320 | tf_op jit(solution)/shard_map/ppermute | solution.py:107
  124.6 2.3 collective-permute-start.30
  128.3 3.6 %shard_map.101 = (bf16[160,2048]{1,0:T(8,128)(2,1)S(1)}, bf16[160,2048]{1,0:T(8,128)(2,1)S(1)}) custom-call(s32[4]{0:T(128)S(1)} %pad_add_fusion.idx_ref, bf16[288,1024]{1,0:T(8,128)(2,1)} %pad_maximum_fusion.rest_0_.rest_2_, bf16[288,1024]{1,0:T(8,128)(2,1)} %collective-permute-done.15.rest_1_.rest_3_, bf16[256,1024]{1,0:T(8,128)(2,1)} %pad_maximum_fusion.9.rest_2_, ...), custom_call_target="tpu_custom_call" | custom-call | flops 1 | bytes 1 | tf_op jit(solution)/shard_map/pallas_call | solution.py:378
  136.3 13.9 %collective-permute-done.30 = bf16[144,2048]{1,0:T(8,128)(2,1)S(1)} collective-permute-done((bf16[144,2048]{1,0:T(8,128)(2,1)}, bf16[144,2048]{1,0:T(8,128)(2,1)S(1)}, u32[]{:S(2)}, u32[]{:S(2)}) %collective-permute-start.30) | collective-permute-done | bytes 589856 | tf_op jit(solution)/shard_map/ppermute | solution.py:107
  150.7 3.3 shard_map.102.rest_0_.hs_ref
  154.0 10.6 %shard_map.103 = (bf16[160,2048]{1,0:T(8,128)(2,1)S(1)}, bf16[160,2048]{1,0:T(8,128)(2,1)S(1)}) custom-call(bf16[160,2048]{1,0:T(8,128)(2,1)S(1)} %get-tuple-element.49.mine_ref, bf16[160,2048]{1,0:T(8,128)(2,1)S(1)} %collective-permute-done.19.other_ref, bf16[128,2,16,1408]{3,2,1,0:T(8,128)(2,1)} %bitcast.52, bf16[1408,2048]{1,0:T(8,128)(2,1)} %bitcast.56, ...), custom_call_target="tpu_custom_call" | custom-call | flops 1 | bytes 1 | tf_op jit(solution)/shard_map/pallas_call | solution.py:378
  166.9 4.3 %shard_map.104 = (f32[256,1024]{1,0:T(8,128)S(1)}, bf16[256,1024]{1,0:T(8,128)(2,1)S(1)}, f32[256,1024]{1,0:T(8,128)S(1)}, bf16[256,1024]{1,0:T(8,128)(2,1)S(1)}) custom-call(s32[4]{0:T(128)S(1)} %pad_add_fusion.idx_ref, bf16[160,2048]{1,0:T(8,128)(2,1)S(1)} %get-tuple-element.52.mine_ref, bf16[160,2048]{1,0:T(8,128)(2,1)S(1)} %collective-permute-done.25.other_ref, ...), custom_call_target="tpu_custom_call" | custom-call | flops 1 | bytes 1 | tf_op jit(solution)/shard_map/pallas_call | solution.py:378
  171.2 2.5 shard_map.105
  178.4 2.9 shard_map.106.rest_0_.hs_ref
  181.4 10.4 %shard_map.107 = (bf16[160,2048]{1,0:T(8,128)(2,1)S(1)}, bf16[160,2048]{1,0:T(8,128)(2,1)S(1)}) custom-call(bf16[160,2048]{1,0:T(8,128)(2,1)S(1)} %get-tuple-element.59.mine_ref, bf16[160,2048]{1,0:T(8,128)(2,1)S(1)} %collective-permute-done.40.other_ref, bf16[128,2,16,1408]{3,2,1,0:T(8,128)(2,1)} %bitcast.53, bf16[1408,2048]{1,0:T(8,128)(2,1)} %bitcast.57, ...), custom_call_target="tpu_custom_call" | custom-call | flops 1 | bytes 1 | tf_op jit(solution)/shard_map/pallas_call | solution.py:378
  194.1 7.9 %collective-permute-done.28 = bf16[256,1024]{1,0:T(8,128)(2,1)S(1)} collective-permute-done((bf16[256,1024]{1,0:T(8,128)(2,1)S(1)}, bf16[256,1024]{1,0:T(8,128)(2,1)S(1)}, u32[]{:S(2)}, u32[]{:S(2)}) %collective-permute-start.28) | collective-permute-done | bytes 524320 | tf_op jit(solution)/shard_map/ppermute | solution.py:107
  202.4 5.1 %shard_map.108 = (f32[256,1024]{1,0:T(8,128)S(1)}, bf16[256,1024]{1,0:T(8,128)(2,1)S(1)}, f32[256,1024]{1,0:T(8,128)}, bf16[256,1024]{1,0:T(8,128)(2,1)S(1)}) custom-call(s32[4]{0:T(128)S(1)} %pad_add_fusion.idx_ref, bf16[160,2048]{1,0:T(8,128)(2,1)S(1)} %get-tuple-element.61.mine_ref, bf16[160,2048]{1,0:T(8,128)(2,1)S(1)} %collective-permute-done.41.other_ref, ...), custom_call_target="tpu_custom_call" | custom-call | flops 1 | bytes 1 | tf_op jit(solution)/shard_map/pallas_call | solution.py:378
  207.5 2.5 shard_map.109
  214.5 2.9 shard_map.110.rest_0_.hs_ref
  217.4 10.4 %shard_map.111 = (bf16[160,2048]{1,0:T(8,128)(2,1)S(1)}, bf16[160,2048]{1,0:T(8,128)(2,1)S(1)}) custom-call(bf16[160,2048]{1,0:T(8,128)(2,1)S(1)} %get-tuple-element.65.mine_ref, bf16[160,2048]{1,0:T(8,128)(2,1)S(1)} %collective-permute-done.42.other_ref, bf16[128,2,16,1408]{3,2,1,0:T(8,128)(2,1)} %bitcast.54, bf16[1408,2048]{1,0:T(8,128)(2,1)} %bitcast.58, ...), custom_call_target="tpu_custom_call" | custom-call | flops 1 | bytes 1 | tf_op jit(solution)/shard_map/pallas_call | solution.py:378
  227.9 8.8 %collective-permute-done.45 = bf16[256,1024]{1,0:T(8,128)(2,1)S(1)} collective-permute-done((bf16[256,1024]{1,0:T(8,128)(2,1)S(1)}, bf16[256,1024]{1,0:T(8,128)(2,1)S(1)}, u32[]{:S(2)}, u32[]{:S(2)}) %collective-permute-start.45) | collective-permute-done | bytes 524320 | tf_op jit(solution)/shard_map/ppermute | solution.py:107
  237.5 5.1 %shard_map.112 = (f32[256,1024]{1,0:T(8,128)S(1)}, bf16[256,1024]{1,0:T(8,128)(2,1)S(1)}, f32[256,1024]{1,0:T(8,128)}, bf16[256,1024]{1,0:T(8,128)(2,1)S(1)}) custom-call(s32[4]{0:T(128)S(1)} %pad_add_fusion.idx_ref, bf16[160,2048]{1,0:T(8,128)(2,1)S(1)} %get-tuple-element.67.mine_ref, bf16[160,2048]{1,0:T(8,128)(2,1)S(1)} %collective-permute-done.43.other_ref, ...), custom_call_target="tpu_custom_call" | custom-call | flops 1 | bytes 1 | tf_op jit(solution)/shard_map/pallas_call | solution.py:378
  242.7 2.5 shard_map.113
  249.4 6.1 %collective-permute-done.59 = bf16[128,1024]{1,0:T(8,128)(2,1)S(1)} collective-permute-done((bf16[128,1024]{1,0:T(8,128)(2,1)S(1)}, bf16[128,1024]{1,0:T(8,128)(2,1)S(1)}, u32[]{:S(2)}, u32[]{:S(2)}) %collective-permute-start.59) | collective-permute-done | bytes 262176 | tf_op jit(solution)/shard_map/ppermute | solution.py:107
  256.6 2.9 shard_map.114.rest_0_.hs_ref
  259.5 10.4 %shard_map.115 = (bf16[160,2048]{1,0:T(8,128)(2,1)S(1)}, bf16[160,2048]{1,0:T(8,128)(2,1)S(1)}) custom-call(bf16[160,2048]{1,0:T(8,128)(2,1)S(1)} %get-tuple-element.74.mine_ref, bf16[160,2048]{1,0:T(8,128)(2,1)S(1)} %collective-permute-done.46.other_ref, bf16[128,2,16,1408]{3,2,1,0:T(8,128)(2,1)} %bitcast.55, bf16[1408,2048]{1,0:T(8,128)(2,1)} %bitcast.59, ...), custom_call_target="tpu_custom_call" | custom-call | flops 1 | bytes 1 | tf_op jit(solution)/shard_map/pallas_call | solution.py:378
  273.0 5.1 %shard_map.116 = (f32[256,1024]{1,0:T(8,128)S(1)}, bf16[256,1024]{1,0:T(8,128)(2,1)S(1)}, f32[256,1024]{1,0:T(8,128)}, bf16[256,1024]{1,0:T(8,128)(2,1)S(1)}) custom-call(s32[4]{0:T(128)S(1)} %pad_add_fusion.idx_ref, bf16[160,2048]{1,0:T(8,128)(2,1)S(1)} %get-tuple-element.76.mine_ref, bf16[160,2048]{1,0:T(8,128)(2,1)S(1)} %collective-permute-done.47.other_ref, ...), custom_call_target="tpu_custom_call" | custom-call | flops 1 | bytes 1 | tf_op jit(solution)/shard_map/pallas_call | solution.py:378
  282.8 8.9 %collective-permute-done.52 = bf16[256,1024]{1,0:T(8,128)(2,1)S(1)} collective-permute-done((bf16[256,1024]{1,0:T(8,128)(2,1)S(1)}, bf16[256,1024]{1,0:T(8,128)(2,1)S(1)}, u32[]{:S(2)}, u32[]{:S(2)}) %collective-permute-start.52) | collective-permute-done | bytes 524320 | tf_op jit(solution)/shard_map/ppermute | solution.py:107
  296.1 3.0 collective-permute-done.53
  300.4 3.3 %collective-permute-start.57 = (bf16[128,2048]{1,0:T(8,128)(2,1)S(1)}, bf16[128,2048]{1,0:T(8,128)(2,1)S(1)}, u32[]{:S(2)}, u32[]{:S(2)}) collective-permute-start(bf16[128,2048]{1,0:T(8,128)(2,1)S(1)} %fusion.7), channel_id=1, source_target_pairs={{0,16},{1,17},{2,18},{3,19},{4,20},{5,21},{6,22},{7,23},{8,24},{9,... | collective-permute-start | bytes 1572872 | tf_op jit(solution)/shard_map/ppermute | solution.py:107
  304.7 5.4 %collective-permute-done.27 = bf16[128,1024]{1,0:T(8,128)(2,1)S(1)} collective-permute-done((bf16[128,1024]{1,0:T(8,128)(2,1)S(1)}, bf16[128,1024]{1,0:T(8,128)(2,1)S(1)}, u32[]{:S(2)}, u32[]{:S(2)}) %collective-permute-start.27) | collective-permute-done | bytes 262176 | tf_op jit(solution)/shard_map/ppermute | solution.py:107
  310.1 3.7 %collective-permute-done.60 = bf16[128,2048]{1,0:T(8,128)(2,1)S(1)} collective-permute-done((bf16[128,2048]{1,0:T(8,128)(2,1)S(1)}, bf16[128,2048]{1,0:T(8,128)(2,1)S(1)}, u32[]{:S(2)}, u32[]{:S(2)}) %collective-permute-start.60) | collective-permute-done | bytes 524320 | tf_op jit(solution)/shard_map/ppermute | solution.py:107
  313.8 10.7 %collective-permute-done.57 = bf16[128,2048]{1,0:T(8,128)(2,1)S(1)} collective-permute-done((bf16[128,2048]{1,0:T(8,128)(2,1)S(1)}, bf16[128,2048]{1,0:T(8,128)(2,1)S(1)}, u32[]{:S(2)}, u32[]{:S(2)}) %collective-permute-start.57) | collective-permute-done | bytes 524320 | tf_op jit(solution)/shard_map/ppermute | solution.py:107
  (209 shorter events, 74.5 us)
Async XLA Ops:
  3.6 15.2 %collective-permute-start.2 = (bf16[128,1024]{1,0:T(8,128)(2,1)S(1)}, bf16[128,1024]{1,0:T(8,128)(2,1)}, u32[]{:S(2)}, u32[]{:S(2)}) collective-permute-start(bf16[128,1024]{1,0:T(8,128)(2,1)S(1)} %pad_maximum_fusion.15), channel_id=1, source_target_pairs={{0,8},{1,9},{2,10},{3,11},{4,12},{5,13},{6,14},{7,15},{8,0},{9,1},... | collective-permute-start | bytes 786440 | tf_op jit(solution)/shard_map/ppermute | solution.py:107
  6.6 14.6 %collective-permute-start.7 = (bf16[128,1024]{1,0:T(8,128)(2,1)S(1)}, bf16[128,1024]{1,0:T(8,128)(2,1)S(1)}, u32[]{:S(2)}, u32[]{:S(2)}) collective-permute-start(bf16[128,1024]{1,0:T(8,128)(2,1)S(1)} %pad_maximum_fusion.15), channel_id=1, source_target_pairs={{0,16},{1,17},{2,18},{3,19},{4,20},{5,21},{6,22},{7,23},{8,24},{9,... | collective-permute-start | bytes 786440 | tf_op jit(solution)/shard_map/ppermute | solution.py:107
  21.7 10.8 %collective-permute-start.3 = (bf16[256,512]{1,0:T(8,128)(2,1)S(1)}, bf16[256,512]{1,0:T(8,128)(2,1)S(1)}, u32[]{:S(2)}, u32[]{:S(2)}) collective-permute-start(bf16[256,512]{1,0:T(8,128)(2,1)S(1)} %get-tuple-element.90), channel_id=1, source_target_pairs={{0,2},{1,3},{2,0},{3,1},{4,6},{5,7},{6,4},{7,5},{8,10},{9,11},{10,... | collective-permute-start | bytes 786440 | tf_op jit(solution)/shard_map/ppermute | solution.py:107
  23.3 9.2 %collective-permute-start.5 = (bf16[256,512]{1,0:T(8,128)(2,1)S(1)}, bf16[256,512]{1,0:T(8,128)(2,1)S(1)}, u32[]{:S(2)}, u32[]{:S(2)}) collective-permute-start(bf16[256,512]{1,0:T(8,128)(2,1)S(1)} %get-tuple-element.89), channel_id=1, source_target_pairs={{0,4},{1,5},{2,6},{3,7},{4,0},{5,1},{6,2},{7,3},{8,12},{9,13},{10,... | collective-permute-start | bytes 786440 | tf_op jit(solution)/shard_map/ppermute | solution.py:107
  38.2 60.0 %all-to-all-start = ((bf16[32,3,64,128]{3,2,1,0:T(8,128)(2,1)}), bf16[32,3,64,128]{3,2,1,0:T(8,128)(2,1)S(1)}, u32[]{:S(2)}, u32[]{:S(2)}) async-start(bf16[32,3,64,128]{3,2,1,0:T(8,128)(2,1)} %fusion.3), calls=%async_computation | async-start | bytes 3145728 | tf_op jit(solution)/shard_map/all_to_all | solution.py:412
  43.1 29.0 %collective-permute-start.4 = (bf16[512,512]{1,0:T(8,128)(2,1)S(1)}, bf16[512,512]{1,0:T(8,128)(2,1)}, u32[]{:S(2)}, u32[]{:S(2)}) collective-permute-start(bf16[512,512]{1,0:T(8,128)(2,1)S(1)} %pad_maximum_fusion.5.rest_0_), channel_id=1, source_target_pairs={{0,4},{1,5},{2,6},{3,7},{4,0},{5,1},{6,2},{7,3},{8,12},{9,13},{10,... | collective-permute-start | bytes 1572872 | tf_op jit(solution)/shard_map/ppermute | solution.py:107
  45.0 27.6 %collective-permute-start.6 = (bf16[512,512]{1,0:T(8,128)(2,1)S(1)}, bf16[512,512]{1,0:T(8,128)(2,1)}, u32[]{:S(2)}, u32[]{:S(2)}) collective-permute-start(bf16[512,512]{1,0:T(8,128)(2,1)S(1)} %pad_maximum_fusion.6.rest_2_), channel_id=1, source_target_pairs={{0,2},{1,3},{2,0},{3,1},{4,6},{5,7},{6,4},{7,5},{8,10},{9,11},{10,... | collective-permute-start | bytes 1572872 | tf_op jit(solution)/shard_map/ppermute | solution.py:107
  46.5 38.9 %collective-permute-start.10 = (bf16[512,512]{1,0:T(8,128)(2,1)S(1)}, bf16[512,512]{1,0:T(8,128)(2,1)}, u32[]{:S(2)}, u32[]{:S(2)}) collective-permute-start(bf16[512,512]{1,0:T(8,128)(2,1)S(1)} %pad_maximum_fusion.7.rest_4_), channel_id=1, source_target_pairs={{0,4},{1,5},{2,6},{3,7},{4,0},{5,1},{6,2},{7,3},{8,12},{9,13},{10,... | collective-permute-start | bytes 1572872 | tf_op jit(solution)/shard_map/ppermute | solution.py:107
  47.0 38.4 %collective-permute-start.12 = (bf16[512,512]{1,0:T(8,128)(2,1)}, bf16[512,512]{1,0:T(8,128)(2,1)}, u32[]{:S(2)}, u32[]{:S(2)}) collective-permute-start(bf16[512,512]{1,0:T(8,128)(2,1)} %pad_maximum_fusion.8.rest_6_), channel_id=1, source_target_pairs={{0,2},{1,3},{2,0},{3,1},{4,6},{5,7},{6,4},{7,5},{8,10},{9,11},{10,... | collective-permute-start | bytes 1572872 | tf_op jit(solution)/shard_map/ppermute | solution.py:107
  49.1 11.4 %collective-permute-start = (bf16[128,1024]{1,0:T(8,128)(2,1)}, bf16[128,1024]{1,0:T(8,128)(2,1)}, u32[]{:S(2)}, u32[]{:S(2)}) collective-permute-start(bf16[128,1024]{1,0:T(8,128)(2,1)} %get-tuple-element.91), channel_id=1, source_target_pairs={{0,1},{1,0},{2,3},{3,2},{4,5},{5,4},{6,7},{7,6},{8,9},{9,8},{10,11... | collective-permute-start | bytes 786440 | tf_op jit(solution)/shard_map/ppermute | solution.py:107
  98.2 30.1 %collective-permute-start.18 = (bf16[32,3,64,128]{3,2,1,0:T(8,128)(2,1)S(1)}, bf16[32,3,64,128]{3,2,1,0:T(8,128)(2,1)S(1)}, u32[]{:S(2)}, u32[]{:S(2)}) collective-permute-start(bf16[32,3,64,128]{3,2,1,0:T(8,128)(2,1)S(1)} %all-to-all-done.three_ref.rest_0_), channel_id=1, source_target_pairs={{0,1},{1,0},{2,3},{3,2},{4,5},{5,4},{6,7},{7,6},{8,9},{9,8},{10,11... | collective-permute-start | bytes 4718600 | tf_op jit(solution)/shard_map/ppermute | solution.py:107
  101.7 9.1 %collective-permute-start.14 = (bf16[144,1024]{1,0:T(8,128)(2,1)S(1)}, bf16[144,1024]{1,0:T(8,128)(2,1)S(1)}, u32[]{:S(2)}, u32[]{:S(2)}) collective-permute-start(bf16[144,1024]{1,0:T(8,128)(2,1)S(1)} %slice.142), channel_id=1, source_target_pairs={{0,2},{1,3},{2,0},{3,1},{4,6},{5,7},{6,4},{7,5},{8,10},{9,11},{10,... | collective-permute-start | bytes 884744 | tf_op jit(solution)/shard_map/ppermute | solution.py:107
  102.4 14.8 %collective-permute-start.20 = (bf16[144,2048]{1,0:T(8,128)(2,1)S(1)}, bf16[144,2048]{1,0:T(8,128)(2,1)S(1)}, u32[]{:S(2)}, u32[]{:S(2)}) collective-permute-start(bf16[144,2048]{1,0:T(8,128)(2,1)S(1)} %fusion.10), channel_id=1, source_target_pairs={{0,8},{1,9},{2,10},{3,11},{4,12},{5,13},{6,14},{7,15},{8,0},{9,1},... | collective-permute-start | bytes 1769480 | tf_op jit(solution)/shard_map/ppermute | solution.py:107
  109.4 15.2 %collective-permute-start.17 = (bf16[256,1024]{1,0:T(8,128)(2,1)}, bf16[256,1024]{1,0:T(8,128)(2,1)}, u32[]{:S(2)}, u32[]{:S(2)}) collective-permute-start(bf16[256,1024]{1,0:T(8,128)(2,1)} %pad_maximum_fusion.9.rest_2_), channel_id=1, source_target_pairs={{0,2},{1,3},{2,0},{3,1},{4,6},{5,7},{6,4},{7,5},{8,10},{9,11},{10,... | collective-permute-start | bytes 1572872 | tf_op jit(solution)/shard_map/ppermute | solution.py:107
  111.7 16.6 %collective-permute-start.15 = (bf16[288,1024]{1,0:T(8,128)(2,1)}, bf16[288,1024]{1,0:T(8,128)(2,1)}, u32[]{:S(2)}, u32[]{:S(2)}) collective-permute-start(bf16[288,1024]{1,0:T(8,128)(2,1)} %pad_maximum_fusion.rest_0_.rest_2_), channel_id=1, source_target_pairs={{0,4},{1,5},{2,6},{3,7},{4,0},{5,1},{6,2},{7,3},{8,12},{9,13},{10,... | collective-permute-start | bytes 1769480 | tf_op jit(solution)/shard_map/ppermute | solution.py:107
  117.9 14.1 %collective-permute-start.21 = (bf16[144,1024]{1,0:T(8,128)(2,1)}, bf16[144,1024]{1,0:T(8,128)(2,1)}, u32[]{:S(2)}, u32[]{:S(2)}) collective-permute-start(bf16[144,1024]{1,0:T(8,128)(2,1)} %slice.144), channel_id=1, source_target_pairs={{0,2},{1,3},{2,0},{3,1},{4,6},{5,7},{6,4},{7,5},{8,10},{9,11},{10,... | collective-permute-start | bytes 884744 | tf_op jit(solution)/shard_map/ppermute | solution.py:107
  120.1 13.6 %collective-permute-start.22 = (bf16[128,1024]{1,0:T(8,128)(2,1)}, bf16[128,1024]{1,0:T(8,128)(2,1)}, u32[]{:S(2)}, u32[]{:S(2)}) collective-permute-start(bf16[128,1024]{1,0:T(8,128)(2,1)} %slice.145), channel_id=1, source_target_pairs={{0,4},{1,5},{2,6},{3,7},{4,0},{5,1},{6,2},{7,3},{8,12},{9,13},{10,... | collective-permute-start | bytes 786440 | tf_op jit(solution)/shard_map/ppermute | solution.py:107
  124.6 25.6 %collective-permute-start.30 = (bf16[144,2048]{1,0:T(8,128)(2,1)}, bf16[144,2048]{1,0:T(8,128)(2,1)S(1)}, u32[]{:S(2)}, u32[]{:S(2)}) collective-permute-start(bf16[144,2048]{1,0:T(8,128)(2,1)} %copy-done.11), channel_id=1, source_target_pairs={{0,16},{1,17},{2,18},{3,19},{4,20},{5,21},{6,22},{7,23},{8,24},{9,... | collective-permute-start | bytes 1769480 | tf_op jit(solution)/shard_map/ppermute | solution.py:107
  131.9 22.1 %collective-permute-start.19 = (bf16[160,2048]{1,0:T(8,128)(2,1)S(1)}, bf16[160,2048]{1,0:T(8,128)(2,1)S(1)}, u32[]{:S(2)}, u32[]{:S(2)}) collective-permute-start(bf16[160,2048]{1,0:T(8,128)(2,1)S(1)} %get-tuple-element.50.rest_4_), channel_id=1, source_target_pairs={{0,1},{1,0},{2,3},{3,2},{4,5},{5,4},{6,7},{7,6},{8,9},{9,8},{10,11... | collective-permute-start | bytes 1966088 | tf_op jit(solution)/shard_map/ppermute | solution.py:107
  133.1 31.5 %collective-permute-start.23 = (bf16[288,1024]{1,0:T(8,128)(2,1)S(1)}, bf16[288,1024]{1,0:T(8,128)(2,1)S(1)}, u32[]{:S(2)}, u32[]{:S(2)}) collective-permute-start(bf16[288,1024]{1,0:T(8,128)(2,1)S(1)} %pad_maximum_fusion.1.rest_1_.rest_0_.rest_2_), channel_id=1, source_target_pairs={{0,4},{1,5},{2,6},{3,7},{4,0},{5,1},{6,2},{7,3},{8,12},{9,13},{10,... | collective-permute-start | bytes 1769480 | tf_op jit(solution)/shard_map/ppermute | solution.py:107
  134.7 29.8 %collective-permute-start.24 = (bf16[256,1024]{1,0:T(8,128)(2,1)S(1)}, bf16[256,1024]{1,0:T(8,128)(2,1)S(1)}, u32[]{:S(2)}, u32[]{:S(2)}) collective-permute-start(bf16[256,1024]{1,0:T(8,128)(2,1)S(1)} %pad_maximum_fusion.10.rest_2_), channel_id=1, source_target_pairs={{0,2},{1,3},{2,0},{3,1},{4,6},{5,7},{6,4},{7,5},{8,10},{9,11},{10,... | collective-permute-start | bytes 1572872 | tf_op jit(solution)/shard_map/ppermute | solution.py:107
  150.2 14.5 %collective-permute-start.35 = (bf16[144,2048]{1,0:T(8,128)(2,1)S(1)}, bf16[144,2048]{1,0:T(8,128)(2,1)S(1)}, u32[]{:S(2)}, u32[]{:S(2)}) collective-permute-start(bf16[144,2048]{1,0:T(8,128)(2,1)S(1)} %collective-permute-done.30), channel_id=1, source_target_pairs={{0,8},{1,9},{2,10},{3,11},{4,12},{5,13},{6,14},{7,15},{8,0},{9,1},... | collective-permute-start | bytes 1769480 | tf_op jit(solution)/shard_map/ppermute | solution.py:107
  164.7 9.5 %collective-permute-start.36 = (bf16[144,1024]{1,0:T(8,128)(2,1)S(1)}, bf16[144,1024]{1,0:T(8,128)(2,1)S(1)}, u32[]{:S(2)}, u32[]{:S(2)}) collective-permute-start(bf16[144,1024]{1,0:T(8,128)(2,1)S(1)} %slice.152), channel_id=1, source_target_pairs={{0,2},{1,3},{2,0},{3,1},{4,6},{5,7},{6,4},{7,5},{8,10},{9,11},{10,... | collective-permute-start | bytes 884744 | tf_op jit(solution)/shard_map/ppermute | solution.py:107
  166.3 9.5 %collective-permute-start.38 = (bf16[128,1024]{1,0:T(8,128)(2,1)S(1)}, bf16[128,1024]{1,0:T(8,128)(2,1)S(1)}, u32[]{:S(2)}, u32[]{:S(2)}) collective-permute-start(bf16[128,1024]{1,0:T(8,128)(2,1)S(1)} %slice.153), channel_id=1, source_target_pairs={{0,4},{1,5},{2,6},{3,7},{4,0},{5,1},{6,2},{7,3},{8,12},{9,13},{10,... | collective-permute-start | bytes 786440 | tf_op jit(solution)/shard_map/ppermute | solution.py:107
  174.2 17.5 %collective-permute-start.37 = (bf16[288,1024]{1,0:T(8,128)(2,1)S(1)}, bf16[288,1024]{1,0:T(8,128)(2,1)S(1)}, u32[]{:S(2)}, u32[]{:S(2)}) collective-permute-start(bf16[288,1024]{1,0:T(8,128)(2,1)S(1)} %pad_maximum_fusion.3.rest_1_.rest_0_.rest_2_), channel_id=1, source_target_pairs={{0,4},{1,5},{2,6},{3,7},{4,0},{5,1},{6,2},{7,3},{8,12},{9,13},{10,... | collective-permute-start | bytes 1769480 | tf_op jit(solution)/shard_map/ppermute | solution.py:107
  175.8 15.9 %collective-permute-start.39 = (bf16[256,1024]{1,0:T(8,128)(2,1)S(1)}, bf16[256,1024]{1,0:T(8,128)(2,1)S(1)}, u32[]{:S(2)}, u32[]{:S(2)}) collective-permute-start(bf16[256,1024]{1,0:T(8,128)(2,1)S(1)} %pad_maximum_fusion.12.rest_2_), channel_id=1, source_target_pairs={{0,2},{1,3},{2,0},{3,1},{4,6},{5,7},{6,4},{7,5},{8,10},{9,11},{10,... | collective-permute-start | bytes 1572872 | tf_op jit(solution)/shard_map/ppermute | solution.py:107
  176.4 25.5 %collective-permute-start.28 = (bf16[256,1024]{1,0:T(8,128)(2,1)S(1)}, bf16[256,1024]{1,0:T(8,128)(2,1)S(1)}, u32[]{:S(2)}, u32[]{:S(2)}) collective-permute-start(bf16[256,1024]{1,0:T(8,128)(2,1)S(1)} %get-tuple-element.58), channel_id=1, source_target_pairs={{0,2},{1,3},{2,0},{3,1},{4,6},{5,7},{6,4},{7,5},{8,10},{9,11},{10,... | collective-permute-start | bytes 1572872 | tf_op jit(solution)/shard_map/ppermute | solution.py:107
  177.9 24.2 %collective-permute-start.26 = (bf16[256,1024]{1,0:T(8,128)(2,1)S(1)}, bf16[256,1024]{1,0:T(8,128)(2,1)S(1)}, u32[]{:S(2)}, u32[]{:S(2)}) collective-permute-start(bf16[256,1024]{1,0:T(8,128)(2,1)S(1)} %get-tuple-element.56.rest_4_), channel_id=1, source_target_pairs={{0,4},{1,5},{2,6},{3,7},{4,0},{5,1},{6,2},{7,3},{8,12},{9,13},{10,... | collective-permute-start | bytes 1572872 | tf_op jit(solution)/shard_map/ppermute | solution.py:107
  191.8 10.6 %collective-permute-start.41 = (bf16[160,2048]{1,0:T(8,128)(2,1)S(1)}, bf16[160,2048]{1,0:T(8,128)(2,1)S(1)}, u32[]{:S(2)}, u32[]{:S(2)}) collective-permute-start(bf16[160,2048]{1,0:T(8,128)(2,1)S(1)} %get-tuple-element.63), channel_id=1, source_target_pairs={{0,1},{1,0},{2,3},{3,2},{4,5},{5,4},{6,7},{7,6},{8,9},{9,8},{10,11... | collective-permute-start | bytes 1966088 | tf_op jit(solution)/shard_map/ppermute | solution.py:107
  191.9 18.3 %collective-permute-start.31 = (bf16[144,1024]{1,0:T(8,128)(2,1)S(1)}, bf16[144,1024]{1,0:T(8,128)(2,1)S(1)}, u32[]{:S(2)}, u32[]{:S(2)}) collective-permute-start(bf16[144,1024]{1,0:T(8,128)(2,1)S(1)} %slice.150), channel_id=1, source_target_pairs={{0,2},{1,3},{2,0},{3,1},{4,6},{5,7},{6,4},{7,5},{8,10},{9,11},{10,... | collective-permute-start | bytes 884744 | tf_op jit(solution)/shard_map/ppermute | solution.py:107
  193.4 17.9 %collective-permute-start.33 = (bf16[128,1024]{1,0:T(8,128)(2,1)S(1)}, bf16[128,1024]{1,0:T(8,128)(2,1)S(1)}, u32[]{:S(2)}, u32[]{:S(2)}) collective-permute-start(bf16[128,1024]{1,0:T(8,128)(2,1)S(1)} %slice.151), channel_id=1, source_target_pairs={{0,4},{1,5},{2,6},{3,7},{4,0},{5,1},{6,2},{7,3},{8,12},{9,13},{10,... | collective-permute-start | bytes 786440 | tf_op jit(solution)/shard_map/ppermute | solution.py:107
  210.2 17.6 %collective-permute-start.32 = (bf16[288,1024]{1,0:T(8,128)(2,1)S(1)}, bf16[288,1024]{1,0:T(8,128)(2,1)S(1)}, u32[]{:S(2)}, u32[]{:S(2)}) collective-permute-start(bf16[288,1024]{1,0:T(8,128)(2,1)S(1)} %pad_maximum_fusion.2.rest_1_.rest_0_.rest_2_), channel_id=1, source_target_pairs={{0,4},{1,5},{2,6},{3,7},{4,0},{5,1},{6,2},{7,3},{8,12},{9,13},{10,... | collective-permute-start | bytes 1769480 | tf_op jit(solution)/shard_map/ppermute | solution.py:107
  211.4 16.4 %collective-permute-start.34 = (bf16[256,1024]{1,0:T(8,128)(2,1)S(1)}, bf16[256,1024]{1,0:T(8,128)(2,1)S(1)}, u32[]{:S(2)}, u32[]{:S(2)}) collective-permute-start(bf16[256,1024]{1,0:T(8,128)(2,1)S(1)} %pad_maximum_fusion.11.rest_2_), channel_id=1, source_target_pairs={{0,2},{1,3},{2,0},{3,1},{4,6},{5,7},{6,4},{7,5},{8,10},{9,11},{10,... | collective-permute-start | bytes 1572872 | tf_op jit(solution)/shard_map/ppermute | solution.py:107
  212.4 24.3 %collective-permute-start.45 = (bf16[256,1024]{1,0:T(8,128)(2,1)S(1)}, bf16[256,1024]{1,0:T(8,128)(2,1)S(1)}, u32[]{:S(2)}, u32[]{:S(2)}) collective-permute-start(bf16[256,1024]{1,0:T(8,128)(2,1)S(1)} %get-tuple-element.72), channel_id=1, source_target_pairs={{0,2},{1,3},{2,0},{3,1},{4,6},{5,7},{6,4},{7,5},{8,10},{9,11},{10,... | collective-permute-start | bytes 1572872 | tf_op jit(solution)/shard_map/ppermute | solution.py:107
  213.5 23.8 %collective-permute-start.44 = (bf16[256,1024]{1,0:T(8,128)(2,1)S(1)}, bf16[256,1024]{1,0:T(8,128)(2,1)S(1)}, u32[]{:S(2)}, u32[]{:S(2)}) collective-permute-start(bf16[256,1024]{1,0:T(8,128)(2,1)S(1)} %get-tuple-element.64.rest_4_), channel_id=1, source_target_pairs={{0,4},{1,5},{2,6},{3,7},{4,0},{5,1},{6,2},{7,3},{8,12},{9,13},{10,... | collective-permute-start | bytes 1572872 | tf_op jit(solution)/shard_map/ppermute | solution.py:107
  227.8 9.7 %collective-permute-start.43 = (bf16[160,2048]{1,0:T(8,128)(2,1)S(1)}, bf16[160,2048]{1,0:T(8,128)(2,1)S(1)}, u32[]{:S(2)}, u32[]{:S(2)}) collective-permute-start(bf16[160,2048]{1,0:T(8,128)(2,1)S(1)} %get-tuple-element.69), channel_id=1, source_target_pairs={{0,1},{1,0},{2,3},{3,2},{4,5},{5,4},{6,7},{7,6},{8,9},{9,8},{10,11... | collective-permute-start | bytes 1966088 | tf_op jit(solution)/shard_map/ppermute | solution.py:107
  245.2 14.3 %collective-permute-start.46 = (bf16[160,2048]{1,0:T(8,128)(2,1)S(1)}, bf16[160,2048]{1,0:T(8,128)(2,1)S(1)}, u32[]{:S(2)}, u32[]{:S(2)}) collective-permute-start(bf16[160,2048]{1,0:T(8,128)(2,1)S(1)} %get-tuple-element.75.rest_4_), channel_id=1, source_target_pairs={{0,1},{1,0},{2,3},{3,2},{4,5},{5,4},{6,7},{7,6},{8,9},{9,8},{10,11... | collective-permute-start | bytes 1966088 | tf_op jit(solution)/shard_map/ppermute | solution.py:107
  245.3 24.8 %collective-permute-start.49 = (bf16[256,1024]{1,0:T(8,128)(2,1)S(1)}, bf16[256,1024]{1,0:T(8,128)(2,1)S(1)}, u32[]{:S(2)}, u32[]{:S(2)}) collective-permute-start(bf16[256,1024]{1,0:T(8,128)(2,1)S(1)} %get-tuple-element.80), channel_id=1, source_target_pairs={{0,2},{1,3},{2,0},{3,1},{4,6},{5,7},{6,4},{7,5},{8,10},{9,11},{10,... | collective-permute-start | bytes 1572872 | tf_op jit(solution)/shard_map/ppermute | solution.py:107
  246.4 9.2 %collective-permute-start.59 = (bf16[128,1024]{1,0:T(8,128)(2,1)S(1)}, bf16[128,1024]{1,0:T(8,128)(2,1)S(1)}, u32[]{:S(2)}, u32[]{:S(2)}) collective-permute-start(bf16[128,1024]{1,0:T(8,128)(2,1)S(1)} %slice.210.rest_5_), channel_id=1, source_target_pairs={{0,4},{1,5},{2,6},{3,7},{4,0},{5,1},{6,2},{7,3},{8,12},{9,13},{10,... | collective-permute-start | bytes 786440 | tf_op jit(solution)/shard_map/ppermute | solution.py:107
  247.4 57.3 %collective-permute-start.29 = (bf16[128,1024]{1,0:T(8,128)(2,1)S(1)}, bf16[128,1024]{1,0:T(8,128)(2,1)S(1)}, u32[]{:S(2)}, u32[]{:S(2)}) collective-permute-start(bf16[128,1024]{1,0:T(8,128)(2,1)S(1)} %slice.212.rest_5_), channel_id=1, source_target_pairs={{0,4},{1,5},{2,6},{3,7},{4,0},{5,1},{6,2},{7,3},{8,12},{9,13},{10,... | collective-permute-start | bytes 786440 | tf_op jit(solution)/shard_map/ppermute | solution.py:107
  248.4 24.5 %collective-permute-start.58 = (bf16[128,1024]{1,0:T(8,128)(2,1)S(1)}, bf16[128,1024]{1,0:T(8,128)(2,1)S(1)}, u32[]{:S(2)}, u32[]{:S(2)}) collective-permute-start(bf16[128,1024]{1,0:T(8,128)(2,1)S(1)} %slice.211.rest_4_), channel_id=1, source_target_pairs={{0,2},{1,3},{2,0},{3,1},{4,6},{5,7},{6,4},{7,5},{8,10},{9,11},{10,... | collective-permute-start | bytes 786440 | tf_op jit(solution)/shard_map/ppermute | solution.py:107
  255.5 16.1 %collective-permute-start.48 = (bf16[256,1024]{1,0:T(8,128)(2,1)S(1)}, bf16[256,1024]{1,0:T(8,128)(2,1)S(1)}, u32[]{:S(2)}, u32[]{:S(2)}) collective-permute-start(bf16[256,1024]{1,0:T(8,128)(2,1)S(1)} %get-tuple-element.73.rest_4_), channel_id=1, source_target_pairs={{0,4},{1,5},{2,6},{3,7},{4,0},{5,1},{6,2},{7,3},{8,12},{9,13},{10,... | collective-permute-start | bytes 1572872 | tf_op jit(solution)/shard_map/ppermute | solution.py:107
  270.3 8.9 %collective-permute-start.55 = (bf16[128,1024]{1,0:T(8,128)(2,1)S(1)}, bf16[128,1024]{1,0:T(8,128)(2,1)S(1)}, u32[]{:S(2)}, u32[]{:S(2)}) collective-permute-start(bf16[128,1024]{1,0:T(8,128)(2,1)S(1)} %slice.208.rest_5_), channel_id=1, source_target_pairs={{0,4},{1,5},{2,6},{3,7},{4,0},{5,1},{6,2},{7,3},{8,12},{9,13},{10,... | collective-permute-start | bytes 786440 | tf_op jit(solution)/shard_map/ppermute | solution.py:107
  278.1 13.6 %collective-permute-start.52 = (bf16[256,1024]{1,0:T(8,128)(2,1)S(1)}, bf16[256,1024]{1,0:T(8,128)(2,1)S(1)}, u32[]{:S(2)}, u32[]{:S(2)}) collective-permute-start(bf16[256,1024]{1,0:T(8,128)(2,1)S(1)} %get-tuple-element.84), channel_id=1, source_target_pairs={{0,2},{1,3},{2,0},{3,1},{4,6},{5,7},{6,4},{7,5},{8,10},{9,11},{10,... | collective-permute-start | bytes 1572872 | tf_op jit(solution)/shard_map/ppermute | solution.py:107
  280.2 13.1 %collective-permute-start.50 = (bf16[256,1024]{1,0:T(8,128)(2,1)S(1)}, bf16[256,1024]{1,0:T(8,128)(2,1)S(1)}, u32[]{:S(2)}, u32[]{:S(2)}) collective-permute-start(bf16[256,1024]{1,0:T(8,128)(2,1)S(1)} %get-tuple-element.82), channel_id=1, source_target_pairs={{0,4},{1,5},{2,6},{3,7},{4,0},{5,1},{6,2},{7,3},{8,12},{9,13},{10,... | collective-permute-start | bytes 1572872 | tf_op jit(solution)/shard_map/ppermute | solution.py:107
  281.3 19.0 %collective-permute-start.56 = (bf16[128,2048]{1,0:T(8,128)(2,1)S(1)}, bf16[128,2048]{1,0:T(8,128)(2,1)S(1)}, u32[]{:S(2)}, u32[]{:S(2)}) collective-permute-start(bf16[128,2048]{1,0:T(8,128)(2,1)S(1)} %pad_maximum_fusion.13), channel_id=1, source_target_pairs={{0,8},{1,9},{2,10},{3,11},{4,12},{5,13},{6,14},{7,15},{8,0},{9,1},... | collective-permute-start | bytes 1572872 | tf_op jit(solution)/shard_map/ppermute | solution.py:107
  294.6 19.3 %collective-permute-start.60 = (bf16[128,2048]{1,0:T(8,128)(2,1)S(1)}, bf16[128,2048]{1,0:T(8,128)(2,1)S(1)}, u32[]{:S(2)}, u32[]{:S(2)}) collective-permute-start(bf16[128,2048]{1,0:T(8,128)(2,1)S(1)} %pad_maximum_fusion.14), channel_id=1, source_target_pairs={{0,8},{1,9},{2,10},{3,11},{4,12},{5,13},{6,14},{7,15},{8,0},{9,1},... | collective-permute-start | bytes 1572872 | tf_op jit(solution)/shard_map/ppermute | solution.py:107
  300.4 24.2 %collective-permute-start.57 = (bf16[128,2048]{1,0:T(8,128)(2,1)S(1)}, bf16[128,2048]{1,0:T(8,128)(2,1)S(1)}, u32[]{:S(2)}, u32[]{:S(2)}) collective-permute-start(bf16[128,2048]{1,0:T(8,128)(2,1)S(1)} %fusion.7), channel_id=1, source_target_pairs={{0,16},{1,17},{2,18},{3,19},{4,20},{5,21},{6,22},{7,23},{8,24},{9,... | collective-permute-start | bytes 1572872 | tf_op jit(solution)/shard_map/ppermute | solution.py:107
  (34 other events, 451.5 us)
where the time goes:
time: 332 us; the launch traced here: 326 us
  waiting for transfers between devices  129 us (39%)
  Pallas kernels  89.9 us (27%)
  starting transfers between devices  66.7 us (20%)
  local copies, waits for them, and re-layouts  21 us (6%)
  other arithmetic  17.1 us (5%)
    ppermute x61, waiting for transfers between devices, swap(): return lax.ppermute(x, 'expert', [(i, i ^ bit) for i in range(n)])  129 us
    pallas_call x17, Pallas kernels, call(): pl.pallas_call(body, out_shape=out_shape, in_specs=[kinds[k] for k in in_...  89.9 us
    ppermute x61, starting transfers between devices, swap(): return lax.ppermute(x, 'expert', [(i, i ^ bit) for i in range(n)])  61.8 us
    another operation x1, local copies, waits for them, and re-layouts, whole_rows(): win = expert_in[0].reshape(wide // pack, pack, 2, -1).transpose(0, 2, 1, 3)  11.3 us
  transfers between devices with their start and end apart: 62, of which 29 were waited for; matrix products, arithmetic and copies ran while one was open for 10% of the time, Pallas kernels for 25%

commit v1 on v0

--- a/solution.py
+++ b/solution.py
@@ -511,9 +511,9 @@
     order = [0] + sorted(range(1, layers), key=lambda k: (k != 1, -k))
     firsts, placed, once = {}, [], []
 
-    def first(k):
+    def first(k, *others):
         if k not in firsts:
-            firsts[k] = spread_first(blocks[k], rows)
+            firsts[k] = spread_first(tie(blocks[k], *others) if others else blocks[k], rows)
         return firsts[k]
 
     upcoming = spread_second(*first(0))
@@ -548,7 +548,7 @@
         )
         after = [hs]
         if at + 1 < layers:
-            after += first(order[at + 1])
+            after += first(order[at + 1], *([placed[0][1]] if at == 1 else []))
         done, back = call(
             functools.partial(expert_kernel, len(after)),
             [sds((slots, wide), bf)] * 2,
@@ -570,7 +570,11 @@
         after = []
         if at + 1 < layers:
             upcoming = spread_second(*first(order[at + 1]))
-            back = tie(back, upcoming[1], upcoming[3])
+            back = tie(back, upcoming[1], upcoming[3], *(blocks[2:3] if not at else []))
+        if not at:
+            for j in range(3, layers):
+                if j & (j - 1):
+                    blocks[j] = swap(tie(blocks[j & (j - 1)], done), LAYER * (j & -j))
         if placed:
             once.append(add_first(*placed[-1]))
             after = [once[-1][1], once[-1][3]]

time: 332 us -> 333 us (level)
    ppermute x61, waiting for transfers between devices: 129 us -> 132 us  [swap(): return lax.ppermute(x, 'expert', [(i, i ^ bit) for i in range(n)])]
  transfers between devices with their start and end apart: 62 -> 62, of which waited for: 29 -> 31; matrix products, arithmetic and copies ran while one was open for 10% -> 10% of each run, Pallas kernels for 25% -> 25%
where the time goes in v1:
time: 333 us; the launch traced here: 328 us
  waiting for transfers between devices  132 us (40%)
  Pallas kernels  89.9 us (27%)
  starting transfers between devices  65.2 us (20%)
  local copies, waits for them, and re-layouts  21 us (6%)
  other arithmetic  17.1 us (5%)
    ppermute x61, waiting for transfers between devices, swap(): return lax.ppermute(x, 'expert', [(i, i ^ bit) for i in range(n)])  132 us
    pallas_call x17, Pallas kernels, call(): pl.pallas_call(body, out_shape=out_shape, in_specs=[kinds[k] for k in in_...  89.9 us
    ppermute x61, starting transfers between devices, swap(): return lax.ppermute(x, 'expert', [(i, i ^ bit) for i in range(n)])  60.3 us
    another operation x1, local copies, waits for them, and re-layouts, whole_rows(): win = expert_in[0].reshape(wide // pack, pack, 2, -1).transpose(0, 2, 1, 3)  11.3 us
  transfers between devices with their start and end apart: 62, of which 31 were waited for; matrix products, arithmetic and copies ran while one was open for 10% of the time, Pallas kernels for 25%

profile of v1, /device:TPU:0, one launch (start us, length us, event | category | flops | bytes accessed | tf_op | source)
XLA Modules:
  0.0 328.0 jit_solution(2694805644002244712)
XLA Ops:
  3.6 3.0 collective-permute-start.2
  6.6 2.6 collective-permute-start.7
  10.7 2.4 reshape.19
  13.8 5.0 %collective-permute-done.2 = bf16[128,1024]{1,0:T(8,128)(2,1)} collective-permute-done((bf16[128,1024]{1,0:T(8,128)(2,1)S(1)}, bf16[128,1024]{1,0:T(8,128)(2,1)}, u32[]{:S(2)}, u32[]{:S(2)}) %collective-permute-start.2) | collective-permute-done | bytes 262176 | tf_op jit(solution)/shard_map/ppermute | solution.py:107
  24.8 2.9 collective-permute-done.8
  29.2 1.7 fusion.3
  32.6 2.0 collective-permute-done.9
  34.6 2.7 collective-permute-done.11
  38.2 4.9 %all-to-all-start = ((bf16[32,3,64,128]{3,2,1,0:T(8,128)(2,1)}), bf16[32,3,64,128]{3,2,1,0:T(8,128)(2,1)S(1)}, u32[]{:S(2)}, u32[]{:S(2)}) async-start(bf16[32,3,64,128]{3,2,1,0:T(8,128)(2,1)} %fusion.3), calls=%async_computation | async-start | bytes 3145728 | tf_op jit(solution)/shard_map/all_to_all | solution.py:412
  43.1 1.9 collective-permute-start.4
  47.2 1.9 broadcast_select_fusion
  49.1 11.3 %copy.28 = bf16[128,16,2,1408]{3,1,2,0:T(8,128)(2,1)} copy(bf16[128,16,2,1408]{3,2,1,0:T(2,128)(2,1)} %bitcast.60) | data formatting | bytes 23068672 | tf_op jit(solution)/shard_map/reshape;squeeze | solution.py:463
  60.5 11.6 %collective-permute-done.4.rest_1_ = bf16[512,512]{1,0:T(8,128)(2,1)} collective-permute-done((bf16[512,512]{1,0:T(8,128)(2,1)S(1)}, bf16[512,512]{1,0:T(8,128)(2,1)}, u32[]{:S(2)}, u32[]{:S(2)}) %collective-permute-start.4) | collective-permute-done | bytes 524320 | tf_op jit(solution)/shard_map/ppermute | solution.py:107
  72.6 12.8 %collective-permute-done.10.rest_5_ = bf16[512,512]{1,0:T(8,128)(2,1)} collective-permute-done((bf16[512,512]{1,0:T(8,128)(2,1)S(1)}, bf16[512,512]{1,0:T(8,128)(2,1)}, u32[]{:S(2)}, u32[]{:S(2)}) %collective-permute-start.10) | collective-permute-done | bytes 524320 | tf_op jit(solution)/shard_map/ppermute | solution.py:107
  87.4 5.3 %shard_map.100 = (f32[128,2048]{1,0:T(8,128)S(1)}, f32[128,2048]{1,0:T(8,128)}) custom-call(s32[16]{0:T(128)S(1)} %stack.98.idx_ref, bf16[128,1024]{1,0:T(8,128)(2,1)S(1)} %copy-done.8, bf16[128,1024]{1,0:T(8,128)(2,1)} %collective-permute-done.other_ref, bf16[512,512]{1,0:T(8,128)(2,1)S(1)} %pad_maximum_fusion.5.rest_0_, ...), custom_call_target="tpu_custom_call" | custom-call | flops 1 | bytes 1 | tf_op jit(solution)/shard_map/pallas_call | solution.py:378
  92.8 2.8 collective-permute-done.13
  98.4 1.7 fusion.9
  103.9 5.4 %collective-permute-done.14 = bf16[144,1024]{1,0:T(8,128)(2,1)S(1)} collective-permute-done((bf16[144,1024]{1,0:T(8,128)(2,1)S(1)}, bf16[144,1024]{1,0:T(8,128)(2,1)S(1)}, u32[]{:S(2)}, u32[]{:S(2)}) %collective-permute-start.14) | collective-permute-done | bytes 294944 | tf_op jit(solution)/shard_map/ppermute | solution.py:107
  113.0 4.1 %collective-permute-done.20 = bf16[144,2048]{1,0:T(8,128)(2,1)S(1)} collective-permute-done((bf16[144,2048]{1,0:T(8,128)(2,1)S(1)}, bf16[144,2048]{1,0:T(8,128)(2,1)S(1)}, u32[]{:S(2)}, u32[]{:S(2)}) %collective-permute-start.20) | collective-permute-done | bytes 589856 | tf_op jit(solution)/shard_map/ppermute | solution.py:107
  120.8 6.9 %collective-permute-done.17.rest_3_ = bf16[256,1024]{1,0:T(8,128)(2,1)} collective-permute-done((bf16[256,1024]{1,0:T(8,128)(2,1)}, bf16[256,1024]{1,0:T(8,128)(2,1)}, u32[]{:S(2)}, u32[]{:S(2)}) %collective-permute-start.17) | collective-permute-done | bytes 524320 | tf_op jit(solution)/shard_map/ppermute | solution.py:107
  127.6 2.4 collective-permute-start.25
  130.1 3.6 %shard_map.101 = (bf16[160,2048]{1,0:T(8,128)(2,1)S(1)}, bf16[160,2048]{1,0:T(8,128)(2,1)S(1)}) custom-call(s32[4]{0:T(128)S(1)} %pad_add_fusion.idx_ref, bf16[288,1024]{1,0:T(8,128)(2,1)} %pad_maximum_fusion.rest_0_.rest_2_, bf16[288,1024]{1,0:T(8,128)(2,1)} %collective-permute-done.15.rest_1_.rest_3_, bf16[256,1024]{1,0:T(8,128)(2,1)} %pad_maximum_fusion.9.rest_2_, ...), custom_call_target="tpu_custom_call" | custom-call | flops 1 | bytes 1 | tf_op jit(solution)/shard_map/pallas_call | solution.py:378
  138.0 3.3 shard_map.102.rest_0_.hs_ref
  141.3 10.6 %shard_map.103 = (bf16[160,2048]{1,0:T(8,128)(2,1)S(1)}, bf16[160,2048]{1,0:T(8,128)(2,1)S(1)}) custom-call(bf16[160,2048]{1,0:T(8,128)(2,1)S(1)} %get-tuple-element.51.mine_ref, bf16[160,2048]{1,0:T(8,128)(2,1)S(1)} %collective-permute-done.19.other_ref, bf16[128,2,16,1408]{3,2,1,0:T(8,128)(2,1)} %bitcast.52, bf16[1408,2048]{1,0:T(8,128)(2,1)} %bitcast.56, ...), custom_call_target="tpu_custom_call" | custom-call | flops 1 | bytes 1 | tf_op jit(solution)/shard_map/pallas_call | solution.py:378
  154.8 4.3 %shard_map.104 = (f32[256,1024]{1,0:T(8,128)S(1)}, bf16[256,1024]{1,0:T(8,128)(2,1)S(1)}, f32[256,1024]{1,0:T(8,128)S(1)}, bf16[256,1024]{1,0:T(8,128)(2,1)S(1)}) custom-call(s32[4]{0:T(128)S(1)} %pad_add_fusion.idx_ref, bf16[160,2048]{1,0:T(8,128)(2,1)S(1)} %get-tuple-element.54.mine_ref, bf16[160,2048]{1,0:T(8,128)(2,1)S(1)} %collective-permute-done.26.other_ref, ...), custom_call_target="tpu_custom_call" | custom-call | flops 1 | bytes 1 | tf_op jit(solution)/shard_map/pallas_call | solution.py:378
  159.1 9.4 %collective-permute-done.35 = bf16[144,2048]{1,0:T(8,128)(2,1)S(1)} collective-permute-done((bf16[144,2048]{1,0:T(8,128)(2,1)S(1)}, bf16[144,2048]{1,0:T(8,128)(2,1)S(1)}, u32[]{:S(2)}, u32[]{:S(2)}) %collective-permute-start.35) | collective-permute-done | bytes 589856 | tf_op jit(solution)/shard_map/ppermute | solution.py:107
  170.6 2.5 shard_map.105
  173.3 3.8 %collective-permute-done.36 = bf16[144,1024]{1,0:T(8,128)(2,1)S(1)} collective-permute-done((bf16[144,1024]{1,0:T(8,128)(2,1)S(1)}, bf16[144,1024]{1,0:T(8,128)(2,1)S(1)}, u32[]{:S(2)}, u32[]{:S(2)}) %collective-permute-start.36) | collective-permute-done | bytes 294944 | tf_op jit(solution)/shard_map/ppermute | solution.py:107
  181.4 2.9 shard_map.106.rest_0_.hs_ref
  184.3 10.4 %shard_map.107 = (bf16[160,2048]{1,0:T(8,128)(2,1)S(1)}, bf16[160,2048]{1,0:T(8,128)(2,1)S(1)}) custom-call(bf16[160,2048]{1,0:T(8,128)(2,1)S(1)} %get-tuple-element.63.mine_ref, bf16[160,2048]{1,0:T(8,128)(2,1)S(1)} %collective-permute-done.40.other_ref, bf16[128,2,16,1408]{3,2,1,0:T(8,128)(2,1)} %bitcast.53, bf16[1408,2048]{1,0:T(8,128)(2,1)} %bitcast.57, ...), custom_call_target="tpu_custom_call" | custom-call | flops 1 | bytes 1 | tf_op jit(solution)/shard_map/pallas_call | solution.py:378
  197.0 7.1 %collective-permute-done.29 = bf16[256,1024]{1,0:T(8,128)(2,1)S(1)} collective-permute-done((bf16[256,1024]{1,0:T(8,128)(2,1)S(1)}, bf16[256,1024]{1,0:T(8,128)(2,1)S(1)}, u32[]{:S(2)}, u32[]{:S(2)}) %collective-permute-start.29) | collective-permute-done | bytes 524320 | tf_op jit(solution)/shard_map/ppermute | solution.py:107
  205.0 5.1 %shard_map.108 = (f32[256,1024]{1,0:T(8,128)S(1)}, bf16[256,1024]{1,0:T(8,128)(2,1)S(1)}, f32[256,1024]{1,0:T(8,128)}, bf16[256,1024]{1,0:T(8,128)(2,1)S(1)}) custom-call(s32[4]{0:T(128)S(1)} %pad_add_fusion.idx_ref, bf16[160,2048]{1,0:T(8,128)(2,1)S(1)} %get-tuple-element.65.mine_ref, bf16[160,2048]{1,0:T(8,128)(2,1)S(1)} %collective-permute-done.41.other_ref, ...), custom_call_target="tpu_custom_call" | custom-call | flops 1 | bytes 1 | tf_op jit(solution)/shard_map/pallas_call | solution.py:378
  210.1 2.5 shard_map.109
  217.0 2.9 shard_map.110.rest_0_.hs_ref
  220.0 10.4 %shard_map.111 = (bf16[160,2048]{1,0:T(8,128)(2,1)S(1)}, bf16[160,2048]{1,0:T(8,128)(2,1)S(1)}) custom-call(bf16[160,2048]{1,0:T(8,128)(2,1)S(1)} %get-tuple-element.69.mine_ref, bf16[160,2048]{1,0:T(8,128)(2,1)S(1)} %collective-permute-done.42.other_ref, bf16[128,2,16,1408]{3,2,1,0:T(8,128)(2,1)} %bitcast.54, bf16[1408,2048]{1,0:T(8,128)(2,1)} %bitcast.58, ...), custom_call_target="tpu_custom_call" | custom-call | flops 1 | bytes 1 | tf_op jit(solution)/shard_map/pallas_call | solution.py:378
  230.5 8.7 %collective-permute-done.45 = bf16[256,1024]{1,0:T(8,128)(2,1)S(1)} collective-permute-done((bf16[256,1024]{1,0:T(8,128)(2,1)S(1)}, bf16[256,1024]{1,0:T(8,128)(2,1)S(1)}, u32[]{:S(2)}, u32[]{:S(2)}) %collective-permute-start.45) | collective-permute-done | bytes 524320 | tf_op jit(solution)/shard_map/ppermute | solution.py:107
  240.1 5.1 %shard_map.112 = (f32[256,1024]{1,0:T(8,128)S(1)}, bf16[256,1024]{1,0:T(8,128)(2,1)S(1)}, f32[256,1024]{1,0:T(8,128)}, bf16[256,1024]{1,0:T(8,128)(2,1)S(1)}) custom-call(s32[4]{0:T(128)S(1)} %pad_add_fusion.idx_ref, bf16[160,2048]{1,0:T(8,128)(2,1)S(1)} %get-tuple-element.71.mine_ref, bf16[160,2048]{1,0:T(8,128)(2,1)S(1)} %collective-permute-done.43.other_ref, ...), custom_call_target="tpu_custom_call" | custom-call | flops 1 | bytes 1 | tf_op jit(solution)/shard_map/pallas_call | solution.py:378
  245.2 2.5 shard_map.113
  252.0 6.0 %collective-permute-done.59 = bf16[128,1024]{1,0:T(8,128)(2,1)S(1)} collective-permute-done((bf16[128,1024]{1,0:T(8,128)(2,1)S(1)}, bf16[128,1024]{1,0:T(8,128)(2,1)S(1)}, u32[]{:S(2)}, u32[]{:S(2)}) %collective-permute-start.59) | collective-permute-done | bytes 262176 | tf_op jit(solution)/shard_map/ppermute | solution.py:107
  259.2 2.9 shard_map.114.rest_0_.hs_ref
  262.1 10.4 %shard_map.115 = (bf16[160,2048]{1,0:T(8,128)(2,1)S(1)}, bf16[160,2048]{1,0:T(8,128)(2,1)S(1)}) custom-call(bf16[160,2048]{1,0:T(8,128)(2,1)S(1)} %get-tuple-element.78.mine_ref, bf16[160,2048]{1,0:T(8,128)(2,1)S(1)} %collective-permute-done.46.other_ref, bf16[128,2,16,1408]{3,2,1,0:T(8,128)(2,1)} %bitcast.55, bf16[1408,2048]{1,0:T(8,128)(2,1)} %bitcast.59, ...), custom_call_target="tpu_custom_call" | custom-call | flops 1 | bytes 1 | tf_op jit(solution)/shard_map/pallas_call | solution.py:378
  275.6 5.1 %shard_map.116 = (f32[256,1024]{1,0:T(8,128)S(1)}, bf16[256,1024]{1,0:T(8,128)(2,1)S(1)}, f32[256,1024]{1,0:T(8,128)}, bf16[256,1024]{1,0:T(8,128)(2,1)S(1)}) custom-call(s32[4]{0:T(128)S(1)} %pad_add_fusion.idx_ref, bf16[160,2048]{1,0:T(8,128)(2,1)S(1)} %get-tuple-element.80.mine_ref, bf16[160,2048]{1,0:T(8,128)(2,1)S(1)} %collective-permute-done.47.other_ref, ...), custom_call_target="tpu_custom_call" | custom-call | flops 1 | bytes 1 | tf_op jit(solution)/shard_map/pallas_call | solution.py:378
  284.8 9.5 %collective-permute-done.52 = bf16[256,1024]{1,0:T(8,128)(2,1)S(1)} collective-permute-done((bf16[256,1024]{1,0:T(8,128)(2,1)S(1)}, bf16[256,1024]{1,0:T(8,128)(2,1)S(1)}, u32[]{:S(2)}, u32[]{:S(2)}) %collective-permute-start.52) | collective-permute-done | bytes 524320 | tf_op jit(solution)/shard_map/ppermute | solution.py:107
  298.1 3.6 %collective-permute-done.53 = bf16[128,1024]{1,0:T(8,128)(2,1)S(1)} collective-permute-done((bf16[128,1024]{1,0:T(8,128)(2,1)S(1)}, bf16[128,1024]{1,0:T(8,128)(2,1)S(1)}, u32[]{:S(2)}, u32[]{:S(2)}) %collective-permute-start.53) | collective-permute-done | bytes 262176 | tf_op jit(solution)/shard_map/ppermute | solution.py:107
  302.8 2.4 collective-permute-start.57
  306.3 5.2 %collective-permute-done.28 = bf16[128,1024]{1,0:T(8,128)(2,1)S(1)} collective-permute-done((bf16[128,1024]{1,0:T(8,128)(2,1)S(1)}, bf16[128,1024]{1,0:T(8,128)(2,1)S(1)}, u32[]{:S(2)}, u32[]{:S(2)}) %collective-permute-start.28) | collective-permute-done | bytes 262176 | tf_op jit(solution)/shard_map/ppermute | solution.py:107
  311.6 4.6 %collective-permute-done.60 = bf16[128,2048]{1,0:T(8,128)(2,1)S(1)} collective-permute-done((bf16[128,2048]{1,0:T(8,128)(2,1)S(1)}, bf16[128,2048]{1,0:T(8,128)(2,1)S(1)}, u32[]{:S(2)}, u32[]{:S(2)}) %collective-permute-start.60) | collective-permute-done | bytes 524320 | tf_op jit(solution)/shard_map/ppermute | solution.py:107
  316.3 10.1 %collective-permute-done.57 = bf16[128,2048]{1,0:T(8,128)(2,1)S(1)} collective-permute-done((bf16[128,2048]{1,0:T(8,128)(2,1)S(1)}, bf16[128,2048]{1,0:T(8,128)(2,1)S(1)}, u32[]{:S(2)}, u32[]{:S(2)}) %collective-permute-start.57) | collective-permute-done | bytes 524320 | tf_op jit(solution)/shard_map/ppermute | solution.py:107
  (209 shorter events, 76.2 us)
Async XLA Ops:
  3.6 15.2 %collective-permute-start.2 = (bf16[128,1024]{1,0:T(8,128)(2,1)S(1)}, bf16[128,1024]{1,0:T(8,128)(2,1)}, u32[]{:S(2)}, u32[]{:S(2)}) collective-permute-start(bf16[128,1024]{1,0:T(8,128)(2,1)S(1)} %pad_maximum_fusion.15), channel_id=1, source_target_pairs={{0,8},{1,9},{2,10},{3,11},{4,12},{5,13},{6,14},{7,15},{8,0},{9,1},... | collective-permute-start | bytes 786440 | tf_op jit(solution)/shard_map/ppermute | solution.py:107
  6.6 14.6 %collective-permute-start.7 = (bf16[128,1024]{1,0:T(8,128)(2,1)S(1)}, bf16[128,1024]{1,0:T(8,128)(2,1)S(1)}, u32[]{:S(2)}, u32[]{:S(2)}) collective-permute-start(bf16[128,1024]{1,0:T(8,128)(2,1)S(1)} %pad_maximum_fusion.15), channel_id=1, source_target_pairs={{0,16},{1,17},{2,18},{3,19},{4,20},{5,21},{6,22},{7,23},{8,24},{9,... | collective-permute-start | bytes 786440 | tf_op jit(solution)/shard_map/ppermute | solution.py:107
  21.7 10.8 %collective-permute-start.3 = (bf16[256,512]{1,0:T(8,128)(2,1)S(1)}, bf16[256,512]{1,0:T(8,128)(2,1)S(1)}, u32[]{:S(2)}, u32[]{:S(2)}) collective-permute-start(bf16[256,512]{1,0:T(8,128)(2,1)S(1)} %get-tuple-element.94), channel_id=1, source_target_pairs={{0,2},{1,3},{2,0},{3,1},{4,6},{5,7},{6,4},{7,5},{8,10},{9,11},{10,... | collective-permute-start | bytes 786440 | tf_op jit(solution)/shard_map/ppermute | solution.py:107
  23.3 9.2 %collective-permute-start.5 = (bf16[256,512]{1,0:T(8,128)(2,1)S(1)}, bf16[256,512]{1,0:T(8,128)(2,1)S(1)}, u32[]{:S(2)}, u32[]{:S(2)}) collective-permute-start(bf16[256,512]{1,0:T(8,128)(2,1)S(1)} %get-tuple-element.93), channel_id=1, source_target_pairs={{0,4},{1,5},{2,6},{3,7},{4,0},{5,1},{6,2},{7,3},{8,12},{9,13},{10,... | collective-permute-start | bytes 786440 | tf_op jit(solution)/shard_map/ppermute | solution.py:107
  38.2 60.0 %all-to-all-start = ((bf16[32,3,64,128]{3,2,1,0:T(8,128)(2,1)}), bf16[32,3,64,128]{3,2,1,0:T(8,128)(2,1)S(1)}, u32[]{:S(2)}, u32[]{:S(2)}) async-start(bf16[32,3,64,128]{3,2,1,0:T(8,128)(2,1)} %fusion.3), calls=%async_computation | async-start | bytes 3145728 | tf_op jit(solution)/shard_map/all_to_all | solution.py:412
  43.1 29.0 %collective-permute-start.4 = (bf16[512,512]{1,0:T(8,128)(2,1)S(1)}, bf16[512,512]{1,0:T(8,128)(2,1)}, u32[]{:S(2)}, u32[]{:S(2)}) collective-permute-start(bf16[512,512]{1,0:T(8,128)(2,1)S(1)} %pad_maximum_fusion.5.rest_0_), channel_id=1, source_target_pairs={{0,4},{1,5},{2,6},{3,7},{4,0},{5,1},{6,2},{7,3},{8,12},{9,13},{10,... | collective-permute-start | bytes 1572872 | tf_op jit(solution)/shard_map/ppermute | solution.py:107
  45.0 27.6 %collective-permute-start.6 = (bf16[512,512]{1,0:T(8,128)(2,1)S(1)}, bf16[512,512]{1,0:T(8,128)(2,1)}, u32[]{:S(2)}, u32[]{:S(2)}) collective-permute-start(bf16[512,512]{1,0:T(8,128)(2,1)S(1)} %pad_maximum_fusion.6.rest_2_), channel_id=1, source_target_pairs={{0,2},{1,3},{2,0},{3,1},{4,6},{5,7},{6,4},{7,5},{8,10},{9,11},{10,... | collective-permute-start | bytes 1572872 | tf_op jit(solution)/shard_map/ppermute | solution.py:107
  46.5 38.9 %collective-permute-start.10 = (bf16[512,512]{1,0:T(8,128)(2,1)S(1)}, bf16[512,512]{1,0:T(8,128)(2,1)}, u32[]{:S(2)}, u32[]{:S(2)}) collective-permute-start(bf16[512,512]{1,0:T(8,128)(2,1)S(1)} %pad_maximum_fusion.7.rest_4_), channel_id=1, source_target_pairs={{0,4},{1,5},{2,6},{3,7},{4,0},{5,1},{6,2},{7,3},{8,12},{9,13},{10,... | collective-permute-start | bytes 1572872 | tf_op jit(solution)/shard_map/ppermute | solution.py:107
  47.0 38.4 %collective-permute-start.12 = (bf16[512,512]{1,0:T(8,128)(2,1)}, bf16[512,512]{1,0:T(8,128)(2,1)}, u32[]{:S(2)}, u32[]{:S(2)}) collective-permute-start(bf16[512,512]{1,0:T(8,128)(2,1)} %pad_maximum_fusion.8.rest_6_), channel_id=1, source_target_pairs={{0,2},{1,3},{2,0},{3,1},{4,6},{5,7},{6,4},{7,5},{8,10},{9,11},{10,... | collective-permute-start | bytes 1572872 | tf_op jit(solution)/shard_map/ppermute | solution.py:107
  49.1 11.4 %collective-permute-start = (bf16[128,1024]{1,0:T(8,128)(2,1)}, bf16[128,1024]{1,0:T(8,128)(2,1)}, u32[]{:S(2)}, u32[]{:S(2)}) collective-permute-start(bf16[128,1024]{1,0:T(8,128)(2,1)} %get-tuple-element.95), channel_id=1, source_target_pairs={{0,1},{1,0},{2,3},{3,2},{4,5},{5,4},{6,7},{7,6},{8,9},{9,8},{10,11... | collective-permute-start | bytes 786440 | tf_op jit(solution)/shard_map/ppermute | solution.py:107
  98.2 31.8 %collective-permute-start.18 = (bf16[32,3,64,128]{3,2,1,0:T(8,128)(2,1)S(1)}, bf16[32,3,64,128]{3,2,1,0:T(8,128)(2,1)S(1)}, u32[]{:S(2)}, u32[]{:S(2)}) collective-permute-start(bf16[32,3,64,128]{3,2,1,0:T(8,128)(2,1)S(1)} %all-to-all-done.three_ref.rest_0_), channel_id=1, source_target_pairs={{0,1},{1,0},{2,3},{3,2},{4,5},{5,4},{6,7},{7,6},{8,9},{9,8},{10,11... | collective-permute-start | bytes 4718600 | tf_op jit(solution)/shard_map/ppermute | solution.py:107
  100.2 9.1 %collective-permute-start.14 = (bf16[144,1024]{1,0:T(8,128)(2,1)S(1)}, bf16[144,1024]{1,0:T(8,128)(2,1)S(1)}, u32[]{:S(2)}, u32[]{:S(2)}) collective-permute-start(bf16[144,1024]{1,0:T(8,128)(2,1)S(1)} %slice.142), channel_id=1, source_target_pairs={{0,2},{1,3},{2,0},{3,1},{4,6},{5,7},{6,4},{7,5},{8,10},{9,11},{10,... | collective-permute-start | bytes 884744 | tf_op jit(solution)/shard_map/ppermute | solution.py:107
  101.7 9.9 %collective-permute-start.16 = (bf16[128,1024]{1,0:T(8,128)(2,1)S(1)}, bf16[128,1024]{1,0:T(8,128)(2,1)S(1)}, u32[]{:S(2)}, u32[]{:S(2)}) collective-permute-start(bf16[128,1024]{1,0:T(8,128)(2,1)S(1)} %slice.143), channel_id=1, source_target_pairs={{0,4},{1,5},{2,6},{3,7},{4,0},{5,1},{6,2},{7,3},{8,12},{9,13},{10,... | collective-permute-start | bytes 786440 | tf_op jit(solution)/shard_map/ppermute | solution.py:107
  102.4 14.8 %collective-permute-start.20 = (bf16[144,2048]{1,0:T(8,128)(2,1)S(1)}, bf16[144,2048]{1,0:T(8,128)(2,1)S(1)}, u32[]{:S(2)}, u32[]{:S(2)}) collective-permute-start(bf16[144,2048]{1,0:T(8,128)(2,1)S(1)} %fusion.10), channel_id=1, source_target_pairs={{0,8},{1,9},{2,10},{3,11},{4,12},{5,13},{6,14},{7,15},{8,0},{9,1},... | collective-permute-start | bytes 1769480 | tf_op jit(solution)/shard_map/ppermute | solution.py:107
  110.2 19.8 %collective-permute-start.15 = (bf16[288,1024]{1,0:T(8,128)(2,1)}, bf16[288,1024]{1,0:T(8,128)(2,1)}, u32[]{:S(2)}, u32[]{:S(2)}) collective-permute-start(bf16[288,1024]{1,0:T(8,128)(2,1)} %pad_maximum_fusion.rest_0_.rest_2_), channel_id=1, source_target_pairs={{0,4},{1,5},{2,6},{3,7},{4,0},{5,1},{6,2},{7,3},{8,12},{9,13},{10,... | collective-permute-start | bytes 1769480 | tf_op jit(solution)/shard_map/ppermute | solution.py:107
  112.5 15.2 %collective-permute-start.17 = (bf16[256,1024]{1,0:T(8,128)(2,1)}, bf16[256,1024]{1,0:T(8,128)(2,1)}, u32[]{:S(2)}, u32[]{:S(2)}) collective-permute-start(bf16[256,1024]{1,0:T(8,128)(2,1)} %pad_maximum_fusion.9.rest_2_), channel_id=1, source_target_pairs={{0,2},{1,3},{2,0},{3,1},{4,6},{5,7},{6,4},{7,5},{8,10},{9,11},{10,... | collective-permute-start | bytes 1572872 | tf_op jit(solution)/shard_map/ppermute | solution.py:107
  117.9 15.8 %collective-permute-start.21 = (bf16[144,1024]{1,0:T(8,128)(2,1)}, bf16[144,1024]{1,0:T(8,128)(2,1)}, u32[]{:S(2)}, u32[]{:S(2)}) collective-permute-start(bf16[144,1024]{1,0:T(8,128)(2,1)} %slice.144), channel_id=1, source_target_pairs={{0,2},{1,3},{2,0},{3,1},{4,6},{5,7},{6,4},{7,5},{8,10},{9,11},{10,... | collective-permute-start | bytes 884744 | tf_op jit(solution)/shard_map/ppermute | solution.py:107
  120.1 15.4 %collective-permute-start.22 = (bf16[128,1024]{1,0:T(8,128)(2,1)}, bf16[128,1024]{1,0:T(8,128)(2,1)}, u32[]{:S(2)}, u32[]{:S(2)}) collective-permute-start(bf16[128,1024]{1,0:T(8,128)(2,1)} %slice.145), channel_id=1, source_target_pairs={{0,4},{1,5},{2,6},{3,7},{4,0},{5,1},{6,2},{7,3},{8,12},{9,13},{10,... | collective-permute-start | bytes 786440 | tf_op jit(solution)/shard_map/ppermute | solution.py:107
  127.6 25.0 %collective-permute-start.25 = (bf16[144,2048]{1,0:T(8,128)(2,1)}, bf16[144,2048]{1,0:T(8,128)(2,1)S(1)}, u32[]{:S(2)}, u32[]{:S(2)}) collective-permute-start(bf16[144,2048]{1,0:T(8,128)(2,1)} %copy-done.11), channel_id=1, source_target_pairs={{0,16},{1,17},{2,18},{3,19},{4,20},{5,21},{6,22},{7,23},{8,24},{9,... | collective-permute-start | bytes 1769480 | tf_op jit(solution)/shard_map/ppermute | solution.py:107
  134.8 17.9 %collective-permute-start.23 = (bf16[288,1024]{1,0:T(8,128)(2,1)S(1)}, bf16[288,1024]{1,0:T(8,128)(2,1)S(1)}, u32[]{:S(2)}, u32[]{:S(2)}) collective-permute-start(bf16[288,1024]{1,0:T(8,128)(2,1)S(1)} %pad_maximum_fusion.1.rest_1_.rest_0_.rest_2_), channel_id=1, source_target_pairs={{0,4},{1,5},{2,6},{3,7},{4,0},{5,1},{6,2},{7,3},{8,12},{9,13},{10,... | collective-permute-start | bytes 1769480 | tf_op jit(solution)/shard_map/ppermute | solution.py:107
  136.5 16.2 %collective-permute-start.24 = (bf16[256,1024]{1,0:T(8,128)(2,1)S(1)}, bf16[256,1024]{1,0:T(8,128)(2,1)S(1)}, u32[]{:S(2)}, u32[]{:S(2)}) collective-permute-start(bf16[256,1024]{1,0:T(8,128)(2,1)S(1)} %pad_maximum_fusion.10.rest_2_), channel_id=1, source_target_pairs={{0,2},{1,3},{2,0},{3,1},{4,6},{5,7},{6,4},{7,5},{8,10},{9,11},{10,... | collective-permute-start | bytes 1572872 | tf_op jit(solution)/shard_map/ppermute | solution.py:107
  152.7 15.7 %collective-permute-start.35 = (bf16[144,2048]{1,0:T(8,128)(2,1)S(1)}, bf16[144,2048]{1,0:T(8,128)(2,1)S(1)}, u32[]{:S(2)}, u32[]{:S(2)}) collective-permute-start(bf16[144,2048]{1,0:T(8,128)(2,1)S(1)} %collective-permute-done.25), channel_id=1, source_target_pairs={{0,8},{1,9},{2,10},{3,11},{4,12},{5,13},{6,14},{7,15},{8,0},{9,1},... | collective-permute-start | bytes 1769480 | tf_op jit(solution)/shard_map/ppermute | solution.py:107
  169.1 8.7 %collective-permute-start.38 = (bf16[128,1024]{1,0:T(8,128)(2,1)S(1)}, bf16[128,1024]{1,0:T(8,128)(2,1)S(1)}, u32[]{:S(2)}, u32[]{:S(2)}) collective-permute-start(bf16[128,1024]{1,0:T(8,128)(2,1)S(1)} %slice.123), channel_id=1, source_target_pairs={{0,4},{1,5},{2,6},{3,7},{4,0},{5,1},{6,2},{7,3},{8,12},{9,13},{10,... | collective-permute-start | bytes 786440 | tf_op jit(solution)/shard_map/ppermute | solution.py:107
  173.2 11.1 %collective-permute-start.40 = (bf16[160,2048]{1,0:T(8,128)(2,1)S(1)}, bf16[160,2048]{1,0:T(8,128)(2,1)S(1)}, u32[]{:S(2)}, u32[]{:S(2)}) collective-permute-start(bf16[160,2048]{1,0:T(8,128)(2,1)S(1)} %get-tuple-element.64.rest_4_), channel_id=1, source_target_pairs={{0,1},{1,0},{2,3},{3,2},{4,5},{5,4},{6,7},{7,6},{8,9},{9,8},{10,11... | collective-permute-start | bytes 1966088 | tf_op jit(solution)/shard_map/ppermute | solution.py:107
  177.1 17.5 %collective-permute-start.37 = (bf16[288,1024]{1,0:T(8,128)(2,1)S(1)}, bf16[288,1024]{1,0:T(8,128)(2,1)S(1)}, u32[]{:S(2)}, u32[]{:S(2)}) collective-permute-start(bf16[288,1024]{1,0:T(8,128)(2,1)S(1)} %pad_maximum_fusion.3.rest_1_.rest_0_.rest_2_), channel_id=1, source_target_pairs={{0,4},{1,5},{2,6},{3,7},{4,0},{5,1},{6,2},{7,3},{8,12},{9,13},{10,... | collective-permute-start | bytes 1769480 | tf_op jit(solution)/shard_map/ppermute | solution.py:107
  177.8 16.8 %collective-permute-start.39 = (bf16[256,1024]{1,0:T(8,128)(2,1)S(1)}, bf16[256,1024]{1,0:T(8,128)(2,1)S(1)}, u32[]{:S(2)}, u32[]{:S(2)}) collective-permute-start(bf16[256,1024]{1,0:T(8,128)(2,1)S(1)} %pad_maximum_fusion.12.rest_2_), channel_id=1, source_target_pairs={{0,2},{1,3},{2,0},{3,1},{4,6},{5,7},{6,4},{7,5},{8,10},{9,11},{10,... | collective-permute-start | bytes 1572872 | tf_op jit(solution)/shard_map/ppermute | solution.py:107
  179.3 24.7 %collective-permute-start.29 = (bf16[256,1024]{1,0:T(8,128)(2,1)S(1)}, bf16[256,1024]{1,0:T(8,128)(2,1)S(1)}, u32[]{:S(2)}, u32[]{:S(2)}) collective-permute-start(bf16[256,1024]{1,0:T(8,128)(2,1)S(1)} %get-tuple-element.60), channel_id=1, source_target_pairs={{0,2},{1,3},{2,0},{3,1},{4,6},{5,7},{6,4},{7,5},{8,10},{9,11},{10,... | collective-permute-start | bytes 1572872 | tf_op jit(solution)/shard_map/ppermute | solution.py:107
  179.9 24.8 %collective-permute-start.27 = (bf16[256,1024]{1,0:T(8,128)(2,1)S(1)}, bf16[256,1024]{1,0:T(8,128)(2,1)S(1)}, u32[]{:S(2)}, u32[]{:S(2)}) collective-permute-start(bf16[256,1024]{1,0:T(8,128)(2,1)S(1)} %get-tuple-element.58.rest_4_), channel_id=1, source_target_pairs={{0,4},{1,5},{2,6},{3,7},{4,0},{5,1},{6,2},{7,3},{8,12},{9,13},{10,... | collective-permute-start | bytes 1572872 | tf_op jit(solution)/shard_map/ppermute | solution.py:107
  194.7 10.3 %collective-permute-start.41 = (bf16[160,2048]{1,0:T(8,128)(2,1)S(1)}, bf16[160,2048]{1,0:T(8,128)(2,1)S(1)}, u32[]{:S(2)}, u32[]{:S(2)}) collective-permute-start(bf16[160,2048]{1,0:T(8,128)(2,1)S(1)} %get-tuple-element.67), channel_id=1, source_target_pairs={{0,1},{1,0},{2,3},{3,2},{4,5},{5,4},{6,7},{7,6},{8,9},{9,8},{10,11... | collective-permute-start | bytes 1966088 | tf_op jit(solution)/shard_map/ppermute | solution.py:107
  194.8 18.0 %collective-permute-start.31 = (bf16[144,1024]{1,0:T(8,128)(2,1)S(1)}, bf16[144,1024]{1,0:T(8,128)(2,1)S(1)}, u32[]{:S(2)}, u32[]{:S(2)}) collective-permute-start(bf16[144,1024]{1,0:T(8,128)(2,1)S(1)} %slice.150), channel_id=1, source_target_pairs={{0,2},{1,3},{2,0},{3,1},{4,6},{5,7},{6,4},{7,5},{8,10},{9,11},{10,... | collective-permute-start | bytes 884744 | tf_op jit(solution)/shard_map/ppermute | solution.py:107
  195.4 18.4 %collective-permute-start.33 = (bf16[128,1024]{1,0:T(8,128)(2,1)S(1)}, bf16[128,1024]{1,0:T(8,128)(2,1)S(1)}, u32[]{:S(2)}, u32[]{:S(2)}) collective-permute-start(bf16[128,1024]{1,0:T(8,128)(2,1)S(1)} %slice.151), channel_id=1, source_target_pairs={{0,4},{1,5},{2,6},{3,7},{4,0},{5,1},{6,2},{7,3},{8,12},{9,13},{10,... | collective-permute-start | bytes 786440 | tf_op jit(solution)/shard_map/ppermute | solution.py:107
  212.8 17.6 %collective-permute-start.32 = (bf16[288,1024]{1,0:T(8,128)(2,1)S(1)}, bf16[288,1024]{1,0:T(8,128)(2,1)S(1)}, u32[]{:S(2)}, u32[]{:S(2)}) collective-permute-start(bf16[288,1024]{1,0:T(8,128)(2,1)S(1)} %pad_maximum_fusion.2.rest_1_.rest_0_.rest_2_), channel_id=1, source_target_pairs={{0,4},{1,5},{2,6},{3,7},{4,0},{5,1},{6,2},{7,3},{8,12},{9,13},{10,... | collective-permute-start | bytes 1769480 | tf_op jit(solution)/shard_map/ppermute | solution.py:107
  213.9 16.5 %collective-permute-start.34 = (bf16[256,1024]{1,0:T(8,128)(2,1)S(1)}, bf16[256,1024]{1,0:T(8,128)(2,1)S(1)}, u32[]{:S(2)}, u32[]{:S(2)}) collective-permute-start(bf16[256,1024]{1,0:T(8,128)(2,1)S(1)} %pad_maximum_fusion.11.rest_2_), channel_id=1, source_target_pairs={{0,2},{1,3},{2,0},{3,1},{4,6},{5,7},{6,4},{7,5},{8,10},{9,11},{10,... | collective-permute-start | bytes 1572872 | tf_op jit(solution)/shard_map/ppermute | solution.py:107
  215.0 24.2 %collective-permute-start.45 = (bf16[256,1024]{1,0:T(8,128)(2,1)S(1)}, bf16[256,1024]{1,0:T(8,128)(2,1)S(1)}, u32[]{:S(2)}, u32[]{:S(2)}) collective-permute-start(bf16[256,1024]{1,0:T(8,128)(2,1)S(1)} %get-tuple-element.76), channel_id=1, source_target_pairs={{0,2},{1,3},{2,0},{3,1},{4,6},{5,7},{6,4},{7,5},{8,10},{9,11},{10,... | collective-permute-start | bytes 1572872 | tf_op jit(solution)/shard_map/ppermute | solution.py:107
  215.9 23.9 %collective-permute-start.44 = (bf16[256,1024]{1,0:T(8,128)(2,1)S(1)}, bf16[256,1024]{1,0:T(8,128)(2,1)S(1)}, u32[]{:S(2)}, u32[]{:S(2)}) collective-permute-start(bf16[256,1024]{1,0:T(8,128)(2,1)S(1)} %get-tuple-element.68.rest_4_), channel_id=1, source_target_pairs={{0,4},{1,5},{2,6},{3,7},{4,0},{5,1},{6,2},{7,3},{8,12},{9,13},{10,... | collective-permute-start | bytes 1572872 | tf_op jit(solution)/shard_map/ppermute | solution.py:107
  230.4 9.7 %collective-permute-start.43 = (bf16[160,2048]{1,0:T(8,128)(2,1)S(1)}, bf16[160,2048]{1,0:T(8,128)(2,1)S(1)}, u32[]{:S(2)}, u32[]{:S(2)}) collective-permute-start(bf16[160,2048]{1,0:T(8,128)(2,1)S(1)} %get-tuple-element.73), channel_id=1, source_target_pairs={{0,1},{1,0},{2,3},{3,2},{4,5},{5,4},{6,7},{7,6},{8,9},{9,8},{10,11... | collective-permute-start | bytes 1966088 | tf_op jit(solution)/shard_map/ppermute | solution.py:107
  247.8 14.3 %collective-permute-start.46 = (bf16[160,2048]{1,0:T(8,128)(2,1)S(1)}, bf16[160,2048]{1,0:T(8,128)(2,1)S(1)}, u32[]{:S(2)}, u32[]{:S(2)}) collective-permute-start(bf16[160,2048]{1,0:T(8,128)(2,1)S(1)} %get-tuple-element.79.rest_4_), channel_id=1, source_target_pairs={{0,1},{1,0},{2,3},{3,2},{4,5},{5,4},{6,7},{7,6},{8,9},{9,8},{10,11... | collective-permute-start | bytes 1966088 | tf_op jit(solution)/shard_map/ppermute | solution.py:107
  247.9 24.8 %collective-permute-start.49 = (bf16[256,1024]{1,0:T(8,128)(2,1)S(1)}, bf16[256,1024]{1,0:T(8,128)(2,1)S(1)}, u32[]{:S(2)}, u32[]{:S(2)}) collective-permute-start(bf16[256,1024]{1,0:T(8,128)(2,1)S(1)} %get-tuple-element.84), channel_id=1, source_target_pairs={{0,2},{1,3},{2,0},{3,1},{4,6},{5,7},{6,4},{7,5},{8,10},{9,11},{10,... | collective-permute-start | bytes 1572872 | tf_op jit(solution)/shard_map/ppermute | solution.py:107
  248.8 9.2 %collective-permute-start.59 = (bf16[128,1024]{1,0:T(8,128)(2,1)S(1)}, bf16[128,1024]{1,0:T(8,128)(2,1)S(1)}, u32[]{:S(2)}, u32[]{:S(2)}) collective-permute-start(bf16[128,1024]{1,0:T(8,128)(2,1)S(1)} %slice.208.rest_5_), channel_id=1, source_target_pairs={{0,4},{1,5},{2,6},{3,7},{4,0},{5,1},{6,2},{7,3},{8,12},{9,13},{10,... | collective-permute-start | bytes 786440 | tf_op jit(solution)/shard_map/ppermute | solution.py:107
  249.9 56.3 %collective-permute-start.30 = (bf16[128,1024]{1,0:T(8,128)(2,1)S(1)}, bf16[128,1024]{1,0:T(8,128)(2,1)S(1)}, u32[]{:S(2)}, u32[]{:S(2)}) collective-permute-start(bf16[128,1024]{1,0:T(8,128)(2,1)S(1)} %slice.210.rest_5_), channel_id=1, source_target_pairs={{0,4},{1,5},{2,6},{3,7},{4,0},{5,1},{6,2},{7,3},{8,12},{9,13},{10,... | collective-permute-start | bytes 786440 | tf_op jit(solution)/shard_map/ppermute | solution.py:107
  250.9 24.6 %collective-permute-start.58 = (bf16[128,1024]{1,0:T(8,128)(2,1)S(1)}, bf16[128,1024]{1,0:T(8,128)(2,1)S(1)}, u32[]{:S(2)}, u32[]{:S(2)}) collective-permute-start(bf16[128,1024]{1,0:T(8,128)(2,1)S(1)} %slice.209.rest_4_), channel_id=1, source_target_pairs={{0,2},{1,3},{2,0},{3,1},{4,6},{5,7},{6,4},{7,5},{8,10},{9,11},{10,... | collective-permute-start | bytes 786440 | tf_op jit(solution)/shard_map/ppermute | solution.py:107
  258.0 16.1 %collective-permute-start.48 = (bf16[256,1024]{1,0:T(8,128)(2,1)S(1)}, bf16[256,1024]{1,0:T(8,128)(2,1)S(1)}, u32[]{:S(2)}, u32[]{:S(2)}) collective-permute-start(bf16[256,1024]{1,0:T(8,128)(2,1)S(1)} %get-tuple-element.77.rest_4_), channel_id=1, source_target_pairs={{0,4},{1,5},{2,6},{3,7},{4,0},{5,1},{6,2},{7,3},{8,12},{9,13},{10,... | collective-permute-start | bytes 1572872 | tf_op jit(solution)/shard_map/ppermute | solution.py:107
  272.9 8.8 %collective-permute-start.55 = (bf16[128,1024]{1,0:T(8,128)(2,1)S(1)}, bf16[128,1024]{1,0:T(8,128)(2,1)S(1)}, u32[]{:S(2)}, u32[]{:S(2)}) collective-permute-start(bf16[128,1024]{1,0:T(8,128)(2,1)S(1)} %slice.206.rest_5_), channel_id=1, source_target_pairs={{0,4},{1,5},{2,6},{3,7},{4,0},{5,1},{6,2},{7,3},{8,12},{9,13},{10,... | collective-permute-start | bytes 786440 | tf_op jit(solution)/shard_map/ppermute | solution.py:107
  280.7 13.6 %collective-permute-start.52 = (bf16[256,1024]{1,0:T(8,128)(2,1)S(1)}, bf16[256,1024]{1,0:T(8,128)(2,1)S(1)}, u32[]{:S(2)}, u32[]{:S(2)}) collective-permute-start(bf16[256,1024]{1,0:T(8,128)(2,1)S(1)} %get-tuple-element.88), channel_id=1, source_target_pairs={{0,2},{1,3},{2,0},{3,1},{4,6},{5,7},{6,4},{7,5},{8,10},{9,11},{10,... | collective-permute-start | bytes 1572872 | tf_op jit(solution)/shard_map/ppermute | solution.py:107
  282.7 13.1 %collective-permute-start.50 = (bf16[256,1024]{1,0:T(8,128)(2,1)S(1)}, bf16[256,1024]{1,0:T(8,128)(2,1)S(1)}, u32[]{:S(2)}, u32[]{:S(2)}) collective-permute-start(bf16[256,1024]{1,0:T(8,128)(2,1)S(1)} %get-tuple-element.86), channel_id=1, source_target_pairs={{0,4},{1,5},{2,6},{3,7},{4,0},{5,1},{6,2},{7,3},{8,12},{9,13},{10,... | collective-permute-start | bytes 1572872 | tf_op jit(solution)/shard_map/ppermute | solution.py:107
  283.9 18.8 %collective-permute-start.56 = (bf16[128,2048]{1,0:T(8,128)(2,1)S(1)}, bf16[128,2048]{1,0:T(8,128)(2,1)S(1)}, u32[]{:S(2)}, u32[]{:S(2)}) collective-permute-start(bf16[128,2048]{1,0:T(8,128)(2,1)S(1)} %pad_maximum_fusion.13), channel_id=1, source_target_pairs={{0,8},{1,9},{2,10},{3,11},{4,12},{5,13},{6,14},{7,15},{8,0},{9,1},... | collective-permute-start | bytes 1572872 | tf_op jit(solution)/shard_map/ppermute | solution.py:107
  297.1 19.1 %collective-permute-start.60 = (bf16[128,2048]{1,0:T(8,128)(2,1)S(1)}, bf16[128,2048]{1,0:T(8,128)(2,1)S(1)}, u32[]{:S(2)}, u32[]{:S(2)}) collective-permute-start(bf16[128,2048]{1,0:T(8,128)(2,1)S(1)} %pad_maximum_fusion.14), channel_id=1, source_target_pairs={{0,8},{1,9},{2,10},{3,11},{4,12},{5,13},{6,14},{7,15},{8,0},{9,1},... | collective-permute-start | bytes 1572872 | tf_op jit(solution)/shard_map/ppermute | solution.py:107
  302.8 23.5 %collective-permute-start.57 = (bf16[128,2048]{1,0:T(8,128)(2,1)S(1)}, bf16[128,2048]{1,0:T(8,128)(2,1)S(1)}, u32[]{:S(2)}, u32[]{:S(2)}) collective-permute-start(bf16[128,2048]{1,0:T(8,128)(2,1)S(1)} %fusion.7), channel_id=1, source_target_pairs={{0,16},{1,17},{2,18},{3,19},{4,20},{5,21},{6,22},{7,23},{8,24},{9,... | collective-permute-start | bytes 1572872 | tf_op jit(solution)/shard_map/ppermute | solution.py:107
  (34 other events, 437.9 us)

commit v2 on v0

--- a/solution.py
+++ b/solution.py
@@ -409,19 +409,19 @@
         spread_first(jnp.concatenate([blocks[k] for k in two], axis=0), cut * len(two))
         for two in twos
     ]
-    exchange = lax.all_to_all(
-        tie(exchange, *(v for first in firsts for v in first)),
-        "expert",
-        split_axis=0,
-        concat_axis=0,
-        tiled=True,
-    )
     pieces, chips = [], []
     for two, first in zip(twos, firsts):
         pieces += spread_second(*first)
         for k in two:
             layer = jnp.bitwise_xor(me // LAYER, k)
             chips += [layer * (LAYER // 2) + jnp.bitwise_xor(me % LAYER // 2, q) for q in range(4)]
+    exchange = lax.all_to_all(
+        tie(exchange, *pieces[:4], *firsts[-1]),
+        "expert",
+        split_axis=0,
+        concat_axis=0,
+        tiled=True,
+    )
     mine, before = lax.optimization_barrier((mine, before))
     here = context.shape[0]
     keep, send = call(

time: 332 us -> 332 us (level)
  local copies, waits for them, and re-layouts: 21 us -> 29 us
  waiting for transfers between devices: 129 us -> 121 us
    ppermute x61, waiting for transfers between devices: 129 us -> 121 us  [swap(): return lax.ppermute(x, 'expert', [(i, i ^ bit) for i in range(n)])]
    unnamed x41 -> x49, local copies, waits for them, and re-layouts: 3.04 us -> 6.73 us
    concatenate x4, local copies, waits for them, and re-layouts: 4.61 us -> 8.09 us  [whole_rows(): jnp.concatenate([shared_in.transpose(1, 0, 2), shared_out.T[None]], axis=0)]
  transfers between devices with their start and end apart: 62 -> 62, of which waited for: 29 -> 27; matrix products, arithmetic and copies ran while one was open for 10% -> 11% of each run, Pallas kernels for 25% -> 25%
where the time goes in v2:
time: 332 us; the launch traced here: 326 us
  waiting for transfers between devices  121 us (36%)
  Pallas kernels  89.9 us (27%)
  starting transfers between devices  66.1 us (20%)
  local copies, waits for them, and re-layouts  29 us (9%)
  other arithmetic  17.2 us (5%)
    ppermute x61, waiting for transfers between devices, swap(): return lax.ppermute(x, 'expert', [(i, i ^ bit) for i in range(n)])  121 us
    pallas_call x17, Pallas kernels, call(): pl.pallas_call(body, out_shape=out_shape, in_specs=[kinds[k] for k in in_...  89.9 us
    ppermute x61, starting transfers between devices, swap(): return lax.ppermute(x, 'expert', [(i, i ^ bit) for i in range(n)])  62.1 us
    another operation x1, local copies, waits for them, and re-layouts, whole_rows(): win = expert_in[0].reshape(wide // pack, pack, 2, -1).transpose(0, 2, 1, 3)  11.3 us
    concatenate x4, local copies, waits for them, and re-layouts, whole_rows(): jnp.concatenate([shared_in.transpose(1, 0, 2), shared_out.T[None]], axis=0)  8.09 us
    unnamed x49, local copies, waits for them, and re-layouts  6.73 us
  transfers between devices with their start and end apart: 62, of which 27 were waited for; matrix products, arithmetic and copies ran while one was open for 11% of the time, Pallas kernels for 25%

profile of v2, /device:TPU:0, one launch (start us, length us, event | category | flops | bytes accessed | tf_op | source)
XLA Modules:
  0.0 325.6 jit_solution(11486714730352940550)
XLA Ops:
  3.6 3.0 collective-permute-start.2
  6.6 2.6 collective-permute-start.7
  9.2 9.5 %collective-permute-done.2 = bf16[128,1024]{1,0:T(8,128)(2,1)S(1)} collective-permute-done((bf16[128,1024]{1,0:T(8,128)(2,1)S(1)}, bf16[128,1024]{1,0:T(8,128)(2,1)S(1)}, u32[]{:S(2)}, u32[]{:S(2)}) %collective-permute-start.2) | collective-permute-done | bytes 262176 | tf_op jit(solution)/shard_map/ppermute | solution.py:107
  22.0 4.6 %collective-permute-done.3 = bf16[256,512]{1,0:T(8,128)(2,1)S(1)} collective-permute-done((bf16[256,512]{1,0:T(8,128)(2,1)S(1)}, bf16[256,512]{1,0:T(8,128)(2,1)S(1)}, u32[]{:S(2)}, u32[]{:S(2)}) %collective-permute-start.3) | collective-permute-done | bytes 262176 | tf_op jit(solution)/shard_map/ppermute | solution.py:107
  32.7 4.7 %reshape.19 = bf16[2,64,32,88]{3,2,0,1:T(8,128)(2,1)} reshape(bf16[2,64,2816]{2,0,1:T(2,128)(2,1)} %bitcast.63) | data formatting | bytes 1441792 | tf_op jit(solution)/shard_map/concatenate | solution.py:471
  37.4 1.9 copy.21
  42.2 3.7 %collective-permute-done.9 = bf16[256,512]{1,0:T(8,128)(2,1)} collective-permute-done((bf16[256,512]{1,0:T(8,128)(2,1)}, bf16[256,512]{1,0:T(8,128)(2,1)}, u32[]{:S(2)}, u32[]{:S(2)}) %collective-permute-start.9) | collective-permute-done | bytes 262176 | tf_op jit(solution)/shard_map/ppermute | solution.py:107
  49.5 4.0 %all-to-all-start = ((bf16[32,3,64,128]{3,2,1,0:T(8,128)(2,1)}), bf16[32,3,64,128]{3,2,1,0:T(8,128)(2,1)S(1)}, u32[]{:S(2)}, u32[]{:S(2)}) async-start(bf16[32,3,64,128]{3,2,1,0:T(8,128)(2,1)} %fusion.3), calls=%async_computation | async-start | bytes 3145728 | tf_op jit(solution)/shard_map/all_to_all | solution.py:418
  53.5 1.9 collective-permute-start.10
  56.9 1.8 broadcast_select_fusion
  58.7 11.3 %copy.28 = bf16[128,16,2,1408]{3,1,2,0:T(8,128)(2,1)} copy(bf16[128,16,2,1408]{3,2,1,0:T(2,128)(2,1)} %bitcast.60) | data formatting | bytes 23068672 | tf_op jit(solution)/shard_map/reshape;squeeze | solution.py:463
  70.1 11.8 %collective-permute-done.10.rest_5_ = bf16[512,512]{1,0:T(8,128)(2,1)} collective-permute-done((bf16[512,512]{1,0:T(8,128)(2,1)S(1)}, bf16[512,512]{1,0:T(8,128)(2,1)}, u32[]{:S(2)}, u32[]{:S(2)}) %collective-permute-start.10) | collective-permute-done | bytes 524320 | tf_op jit(solution)/shard_map/ppermute | solution.py:107
  86.5 5.2 %shard_map.100 = (f32[128,2048]{1,0:T(8,128)S(1)}, f32[128,2048]{1,0:T(8,128)}) custom-call(s32[16]{0:T(128)S(1)} %stack.98.idx_ref, bf16[128,1024]{1,0:T(8,128)(2,1)S(1)} %copy-done.8, bf16[128,1024]{1,0:T(8,128)(2,1)} %collective-permute-done.other_ref, bf16[512,512]{1,0:T(8,128)(2,1)S(1)} %pad_maximum_fusion.5.rest_0_, bf16[512,512]{1,0:T(8,128)(2,1)S(1)} %copy-done.10, ...), custom_call_target="tpu_custom_call" | custom-call | flops 1 | bytes 1 | tf_op jit(solution)/shard_map/pallas_call | solution.py:378
  91.8 2.8 collective-permute-done.13
  101.4 2.2 collective-permute-start.20
  103.6 3.9 %collective-permute-done.16 = bf16[128,1024]{1,0:T(8,128)(2,1)S(1)} collective-permute-done((bf16[128,1024]{1,0:T(8,128)(2,1)S(1)}, bf16[128,1024]{1,0:T(8,128)(2,1)S(1)}, u32[]{:S(2)}, u32[]{:S(2)}) %collective-permute-start.16) | collective-permute-done | bytes 262176 | tf_op jit(solution)/shard_map/ppermute | solution.py:107
  108.4 1.8 collective-permute-start.17
  111.4 5.2 %collective-permute-done.20 = bf16[144,2048]{1,0:T(8,128)(2,1)S(1)} collective-permute-done((bf16[144,2048]{1,0:T(8,128)(2,1)S(1)}, bf16[144,2048]{1,0:T(8,128)(2,1)S(1)}, u32[]{:S(2)}, u32[]{:S(2)}) %collective-permute-start.20) | collective-permute-done | bytes 589856 | tf_op jit(solution)/shard_map/ppermute | solution.py:107
  119.9 3.7 %collective-permute-done.17.rest_3_ = bf16[256,1024]{1,0:T(8,128)(2,1)} collective-permute-done((bf16[256,1024]{1,0:T(8,128)(2,1)}, bf16[256,1024]{1,0:T(8,128)(2,1)}, u32[]{:S(2)}, u32[]{:S(2)}) %collective-permute-start.17) | collective-permute-done | bytes 524320 | tf_op jit(solution)/shard_map/ppermute | solution.py:107
  123.6 3.2 collective-permute-start.30
  127.7 3.6 %shard_map.101 = (bf16[160,2048]{1,0:T(8,128)(2,1)S(1)}, bf16[160,2048]{1,0:T(8,128)(2,1)S(1)}) custom-call(s32[4]{0:T(128)S(1)} %pad_add_fusion.idx_ref, bf16[288,1024]{1,0:T(8,128)(2,1)} %pad_maximum_fusion.rest_0_.rest_2_, bf16[288,1024]{1,0:T(8,128)(2,1)} %collective-permute-done.15.rest_1_.rest_3_, bf16[256,1024]{1,0:T(8,128)(2,1)} %pad_maximum_fusion.9.rest_2_, ...), custom_call_target="tpu_custom_call" | custom-call | flops 1 | bytes 1 | tf_op jit(solution)/shard_map/pallas_call | solution.py:378
  135.4 14.9 %collective-permute-done.30 = bf16[144,2048]{1,0:T(8,128)(2,1)S(1)} collective-permute-done((bf16[144,2048]{1,0:T(8,128)(2,1)}, bf16[144,2048]{1,0:T(8,128)(2,1)S(1)}, u32[]{:S(2)}, u32[]{:S(2)}) %collective-permute-start.30) | collective-permute-done | bytes 589856 | tf_op jit(solution)/shard_map/ppermute | solution.py:107
  150.4 3.3 %shard_map.102.rest_0_.hs_ref = bf16[512,256]{1,0:T(8,128)(2,1)S(1)} custom-call(bf16[32,3,64,128]{3,2,1,0:T(8,128)(2,1)S(1)} %all-to-all-done.three_ref.rest_0_, bf16[32,3,64,128]{3,2,1,0:T(8,128)(2,1)} %copy-done.6, bf16[288,1024]{1,0:T(8,128)(2,1)} %pad_maximum_fusion.rest_0_.rest_2_, bf16[288,1024]{1,0:T(8,128)(2,1)} %collective-permute-done.15.rest_1_.rest_3_, ...), custom_call_target="tpu_custom_call" | custom-call | flops 1 | bytes 1 | tf_op jit(solution)/shard_map/pallas_call | solution.py:378
  153.7 10.6 %shard_map.103 = (bf16[160,2048]{1,0:T(8,128)(2,1)S(1)}, bf16[160,2048]{1,0:T(8,128)(2,1)S(1)}) custom-call(bf16[160,2048]{1,0:T(8,128)(2,1)S(1)} %get-tuple-element.49.mine_ref, bf16[160,2048]{1,0:T(8,128)(2,1)S(1)} %collective-permute-done.19.other_ref, bf16[128,2,16,1408]{3,2,1,0:T(8,128)(2,1)} %bitcast.52, bf16[1408,2048]{1,0:T(8,128)(2,1)} %bitcast.56, ...), custom_call_target="tpu_custom_call" | custom-call | flops 1 | bytes 1 | tf_op jit(solution)/shard_map/pallas_call | solution.py:378
  167.0 4.3 %shard_map.104 = (f32[256,1024]{1,0:T(8,128)S(1)}, bf16[256,1024]{1,0:T(8,128)(2,1)S(1)}, f32[256,1024]{1,0:T(8,128)S(1)}, bf16[256,1024]{1,0:T(8,128)(2,1)S(1)}) custom-call(s32[4]{0:T(128)S(1)} %pad_add_fusion.idx_ref, bf16[160,2048]{1,0:T(8,128)(2,1)S(1)} %get-tuple-element.52.mine_ref, bf16[160,2048]{1,0:T(8,128)(2,1)S(1)} %collective-permute-done.25.other_ref, ...), custom_call_target="tpu_custom_call" | custom-call | flops 1 | bytes 1 | tf_op jit(solution)/shard_map/pallas_call | solution.py:378
  171.3 2.5 shard_map.105
  178.2 2.9 shard_map.106.rest_0_.hs_ref
  181.1 10.4 %shard_map.107 = (bf16[160,2048]{1,0:T(8,128)(2,1)S(1)}, bf16[160,2048]{1,0:T(8,128)(2,1)S(1)}) custom-call(bf16[160,2048]{1,0:T(8,128)(2,1)S(1)} %get-tuple-element.59.mine_ref, bf16[160,2048]{1,0:T(8,128)(2,1)S(1)} %collective-permute-done.40.other_ref, bf16[128,2,16,1408]{3,2,1,0:T(8,128)(2,1)} %bitcast.53, bf16[1408,2048]{1,0:T(8,128)(2,1)} %bitcast.57, ...), custom_call_target="tpu_custom_call" | custom-call | flops 1 | bytes 1 | tf_op jit(solution)/shard_map/pallas_call | solution.py:378
  191.6 1.9 collective-permute-start.31
  194.5 6.6 %collective-permute-done.28 = bf16[256,1024]{1,0:T(8,128)(2,1)S(1)} collective-permute-done((bf16[256,1024]{1,0:T(8,128)(2,1)S(1)}, bf16[256,1024]{1,0:T(8,128)(2,1)S(1)}, u32[]{:S(2)}, u32[]{:S(2)}) %collective-permute-start.28) | collective-permute-done | bytes 524320 | tf_op jit(solution)/shard_map/ppermute | solution.py:107
  201.7 5.2 %shard_map.108 = (f32[256,1024]{1,0:T(8,128)S(1)}, bf16[256,1024]{1,0:T(8,128)(2,1)S(1)}, f32[256,1024]{1,0:T(8,128)}, bf16[256,1024]{1,0:T(8,128)(2,1)S(1)}) custom-call(s32[4]{0:T(128)S(1)} %pad_add_fusion.idx_ref, bf16[160,2048]{1,0:T(8,128)(2,1)S(1)} %get-tuple-element.61.mine_ref, bf16[160,2048]{1,0:T(8,128)(2,1)S(1)} %collective-permute-done.41.other_ref, ...), custom_call_target="tpu_custom_call" | custom-call | flops 1 | bytes 1 | tf_op jit(solution)/shard_map/pallas_call | solution.py:378
  206.8 2.5 shard_map.109
  213.8 2.9 shard_map.110.rest_0_.hs_ref
  216.7 10.4 %shard_map.111 = (bf16[160,2048]{1,0:T(8,128)(2,1)S(1)}, bf16[160,2048]{1,0:T(8,128)(2,1)S(1)}) custom-call(bf16[160,2048]{1,0:T(8,128)(2,1)S(1)} %get-tuple-element.65.mine_ref, bf16[160,2048]{1,0:T(8,128)(2,1)S(1)} %collective-permute-done.42.other_ref, bf16[128,2,16,1408]{3,2,1,0:T(8,128)(2,1)} %bitcast.54, bf16[1408,2048]{1,0:T(8,128)(2,1)} %bitcast.58, ...), custom_call_target="tpu_custom_call" | custom-call | flops 1 | bytes 1 | tf_op jit(solution)/shard_map/pallas_call | solution.py:378
  227.2 8.8 %collective-permute-done.45 = bf16[256,1024]{1,0:T(8,128)(2,1)S(1)} collective-permute-done((bf16[256,1024]{1,0:T(8,128)(2,1)S(1)}, bf16[256,1024]{1,0:T(8,128)(2,1)S(1)}, u32[]{:S(2)}, u32[]{:S(2)}) %collective-permute-start.45) | collective-permute-done | bytes 524320 | tf_op jit(solution)/shard_map/ppermute | solution.py:107
  236.8 5.1 %shard_map.112 = (f32[256,1024]{1,0:T(8,128)S(1)}, bf16[256,1024]{1,0:T(8,128)(2,1)S(1)}, f32[256,1024]{1,0:T(8,128)}, bf16[256,1024]{1,0:T(8,128)(2,1)S(1)}) custom-call(s32[4]{0:T(128)S(1)} %pad_add_fusion.idx_ref, bf16[160,2048]{1,0:T(8,128)(2,1)S(1)} %get-tuple-element.67.mine_ref, bf16[160,2048]{1,0:T(8,128)(2,1)S(1)} %collective-permute-done.43.other_ref, ...), custom_call_target="tpu_custom_call" | custom-call | flops 1 | bytes 1 | tf_op jit(solution)/shard_map/pallas_call | solution.py:378
  242.0 2.5 shard_map.113
  244.6 1.9 collective-permute-start.49
  248.7 6.9 %collective-permute-done.59 = bf16[128,1024]{1,0:T(8,128)(2,1)S(1)} collective-permute-done((bf16[128,1024]{1,0:T(8,128)(2,1)S(1)}, bf16[128,1024]{1,0:T(8,128)(2,1)S(1)}, u32[]{:S(2)}, u32[]{:S(2)}) %collective-permute-start.59) | collective-permute-done | bytes 262176 | tf_op jit(solution)/shard_map/ppermute | solution.py:107
  256.7 2.9 shard_map.114.rest_0_.hs_ref
  259.6 10.4 %shard_map.115 = (bf16[160,2048]{1,0:T(8,128)(2,1)S(1)}, bf16[160,2048]{1,0:T(8,128)(2,1)S(1)}) custom-call(bf16[160,2048]{1,0:T(8,128)(2,1)S(1)} %get-tuple-element.74.mine_ref, bf16[160,2048]{1,0:T(8,128)(2,1)S(1)} %collective-permute-done.46.other_ref, bf16[128,2,16,1408]{3,2,1,0:T(8,128)(2,1)} %bitcast.55, bf16[1408,2048]{1,0:T(8,128)(2,1)} %bitcast.59, ...), custom_call_target="tpu_custom_call" | custom-call | flops 1 | bytes 1 | tf_op jit(solution)/shard_map/pallas_call | solution.py:378
  272.3 5.1 %shard_map.116 = (f32[256,1024]{1,0:T(8,128)S(1)}, bf16[256,1024]{1,0:T(8,128)(2,1)S(1)}, f32[256,1024]{1,0:T(8,128)}, bf16[256,1024]{1,0:T(8,128)(2,1)S(1)}) custom-call(s32[4]{0:T(128)S(1)} %pad_add_fusion.idx_ref, bf16[160,2048]{1,0:T(8,128)(2,1)S(1)} %get-tuple-element.76.mine_ref, bf16[160,2048]{1,0:T(8,128)(2,1)S(1)} %collective-permute-done.47.other_ref, ...), custom_call_target="tpu_custom_call" | custom-call | flops 1 | bytes 1 | tf_op jit(solution)/shard_map/pallas_call | solution.py:378
  282.3 9.1 %collective-permute-done.52 = bf16[256,1024]{1,0:T(8,128)(2,1)S(1)} collective-permute-done((bf16[256,1024]{1,0:T(8,128)(2,1)S(1)}, bf16[256,1024]{1,0:T(8,128)(2,1)S(1)}, u32[]{:S(2)}, u32[]{:S(2)}) %collective-permute-start.52) | collective-permute-done | bytes 524320 | tf_op jit(solution)/shard_map/ppermute | solution.py:107
  296.0 3.1 collective-permute-done.53
  300.4 2.8 collective-permute-start.57
  304.5 5.1 %collective-permute-done.27 = bf16[128,1024]{1,0:T(8,128)(2,1)S(1)} collective-permute-done((bf16[128,1024]{1,0:T(8,128)(2,1)S(1)}, bf16[128,1024]{1,0:T(8,128)(2,1)S(1)}, u32[]{:S(2)}, u32[]{:S(2)}) %collective-permute-start.27) | collective-permute-done | bytes 262176 | tf_op jit(solution)/shard_map/ppermute | solution.py:107
  309.7 4.6 %collective-permute-done.60 = bf16[128,2048]{1,0:T(8,128)(2,1)S(1)} collective-permute-done((bf16[128,2048]{1,0:T(8,128)(2,1)S(1)}, bf16[128,2048]{1,0:T(8,128)(2,1)S(1)}, u32[]{:S(2)}, u32[]{:S(2)}) %collective-permute-start.60) | collective-permute-done | bytes 524320 | tf_op jit(solution)/shard_map/ppermute | solution.py:107
  314.3 9.7 %collective-permute-done.57 = bf16[128,2048]{1,0:T(8,128)(2,1)S(1)} collective-permute-done((bf16[128,2048]{1,0:T(8,128)(2,1)S(1)}, bf16[128,2048]{1,0:T(8,128)(2,1)S(1)}, u32[]{:S(2)}, u32[]{:S(2)}) %collective-permute-start.57) | collective-permute-done | bytes 524320 | tf_op jit(solution)/shard_map/ppermute | solution.py:107
  (217 shorter events, 75.1 us)
Async XLA Ops:
  3.6 15.1 %collective-permute-start.2 = (bf16[128,1024]{1,0:T(8,128)(2,1)S(1)}, bf16[128,1024]{1,0:T(8,128)(2,1)S(1)}, u32[]{:S(2)}, u32[]{:S(2)}) collective-permute-start(bf16[128,1024]{1,0:T(8,128)(2,1)S(1)} %pad_maximum_fusion.15), channel_id=1, source_target_pairs={{0,8},{1,9},{2,10},{3,11},{4,12},{5,13},{6,14},{7,15},{8,0},{9,1},... | collective-permute-start | bytes 786440 | tf_op jit(solution)/shard_map/ppermute | solution.py:107
  6.6 15.4 %collective-permute-start.7 = (bf16[128,1024]{1,0:T(8,128)(2,1)S(1)}, bf16[128,1024]{1,0:T(8,128)(2,1)S(1)}, u32[]{:S(2)}, u32[]{:S(2)}) collective-permute-start(bf16[128,1024]{1,0:T(8,128)(2,1)S(1)} %pad_maximum_fusion.15), channel_id=1, source_target_pairs={{0,16},{1,17},{2,18},{3,19},{4,20},{5,21},{6,22},{7,23},{8,24},{9,... | collective-permute-start | bytes 786440 | tf_op jit(solution)/shard_map/ppermute | solution.py:107
  26.7 21.1 %collective-permute-start.4 = (bf16[512,512]{1,0:T(8,128)(2,1)S(1)}, bf16[512,512]{1,0:T(8,128)(2,1)S(1)}, u32[]{:S(2)}, u32[]{:S(2)}) collective-permute-start(bf16[512,512]{1,0:T(8,128)(2,1)S(1)} %pad_maximum_fusion.5.rest_0_), channel_id=1, source_target_pairs={{0,4},{1,5},{2,6},{3,7},{4,0},{5,1},{6,2},{7,3},{8,12},{9,13},{10,... | collective-permute-start | bytes 1572872 | tf_op jit(solution)/shard_map/ppermute | solution.py:107
  28.2 20.4 %collective-permute-start.6 = (bf16[512,512]{1,0:T(8,128)(2,1)S(1)}, bf16[512,512]{1,0:T(8,128)(2,1)S(1)}, u32[]{:S(2)}, u32[]{:S(2)}) collective-permute-start(bf16[512,512]{1,0:T(8,128)(2,1)S(1)} %pad_maximum_fusion.6.rest_2_), channel_id=1, source_target_pairs={{0,2},{1,3},{2,0},{3,1},{4,6},{5,7},{6,4},{7,5},{8,10},{9,11},{10,... | collective-permute-start | bytes 1572872 | tf_op jit(solution)/shard_map/ppermute | solution.py:107
  30.6 15.3 %collective-permute-start.9 = (bf16[256,512]{1,0:T(8,128)(2,1)}, bf16[256,512]{1,0:T(8,128)(2,1)}, u32[]{:S(2)}, u32[]{:S(2)}) collective-permute-start(bf16[256,512]{1,0:T(8,128)(2,1)} %get-tuple-element.88), channel_id=1, source_target_pairs={{0,2},{1,3},{2,0},{3,1},{4,6},{5,7},{6,4},{7,5},{8,10},{9,11},{10,... | collective-permute-start | bytes 786440 | tf_op jit(solution)/shard_map/ppermute | solution.py:107
  49.5 47.7 %all-to-all-start = ((bf16[32,3,64,128]{3,2,1,0:T(8,128)(2,1)}), bf16[32,3,64,128]{3,2,1,0:T(8,128)(2,1)S(1)}, u32[]{:S(2)}, u32[]{:S(2)}) async-start(bf16[32,3,64,128]{3,2,1,0:T(8,128)(2,1)} %fusion.3), calls=%async_computation | async-start | bytes 3145728 | tf_op jit(solution)/shard_map/all_to_all | solution.py:418
  53.5 28.5 %collective-permute-start.10 = (bf16[512,512]{1,0:T(8,128)(2,1)S(1)}, bf16[512,512]{1,0:T(8,128)(2,1)}, u32[]{:S(2)}, u32[]{:S(2)}) collective-permute-start(bf16[512,512]{1,0:T(8,128)(2,1)S(1)} %pad_maximum_fusion.7.rest_4_), channel_id=1, source_target_pairs={{0,4},{1,5},{2,6},{3,7},{4,0},{5,1},{6,2},{7,3},{8,12},{9,13},{10,... | collective-permute-start | bytes 1572872 | tf_op jit(solution)/shard_map/ppermute | solution.py:107
  55.4 27.0 %collective-permute-start.12 = (bf16[512,512]{1,0:T(8,128)(2,1)}, bf16[512,512]{1,0:T(8,128)(2,1)}, u32[]{:S(2)}, u32[]{:S(2)}) collective-permute-start(bf16[512,512]{1,0:T(8,128)(2,1)} %pad_maximum_fusion.8.rest_6_), channel_id=1, source_target_pairs={{0,2},{1,3},{2,0},{3,1},{4,6},{5,7},{6,4},{7,5},{8,10},{9,11},{10,... | collective-permute-start | bytes 1572872 | tf_op jit(solution)/shard_map/ppermute | solution.py:107
  58.7 11.4 %collective-permute-start = (bf16[128,1024]{1,0:T(8,128)(2,1)}, bf16[128,1024]{1,0:T(8,128)(2,1)}, u32[]{:S(2)}, u32[]{:S(2)}) collective-permute-start(bf16[128,1024]{1,0:T(8,128)(2,1)} %get-tuple-element.91), channel_id=1, source_target_pairs={{0,1},{1,0},{2,3},{3,2},{4,5},{5,4},{6,7},{7,6},{8,9},{9,8},{10,11... | collective-permute-start | bytes 786440 | tf_op jit(solution)/shard_map/ppermute | solution.py:107
  97.2 30.5 %collective-permute-start.18 = (bf16[32,3,64,128]{3,2,1,0:T(8,128)(2,1)S(1)}, bf16[32,3,64,128]{3,2,1,0:T(8,128)(2,1)S(1)}, u32[]{:S(2)}, u32[]{:S(2)}) collective-permute-start(bf16[32,3,64,128]{3,2,1,0:T(8,128)(2,1)S(1)} %all-to-all-done.three_ref.rest_0_), channel_id=1, source_target_pairs={{0,1},{1,0},{2,3},{3,2},{4,5},{5,4},{6,7},{7,6},{8,9},{9,8},{10,11... | collective-permute-start | bytes 4718600 | tf_op jit(solution)/shard_map/ppermute | solution.py:107
  99.2 8.4 %collective-permute-start.16 = (bf16[128,1024]{1,0:T(8,128)(2,1)S(1)}, bf16[128,1024]{1,0:T(8,128)(2,1)S(1)}, u32[]{:S(2)}, u32[]{:S(2)}) collective-permute-start(bf16[128,1024]{1,0:T(8,128)(2,1)S(1)} %slice.143), channel_id=1, source_target_pairs={{0,4},{1,5},{2,6},{3,7},{4,0},{5,1},{6,2},{7,3},{8,12},{9,13},{10,... | collective-permute-start | bytes 786440 | tf_op jit(solution)/shard_map/ppermute | solution.py:107
  100.3 10.0 %collective-permute-start.14 = (bf16[144,1024]{1,0:T(8,128)(2,1)S(1)}, bf16[144,1024]{1,0:T(8,128)(2,1)S(1)}, u32[]{:S(2)}, u32[]{:S(2)}) collective-permute-start(bf16[144,1024]{1,0:T(8,128)(2,1)S(1)} %slice.142), channel_id=1, source_target_pairs={{0,2},{1,3},{2,0},{3,1},{4,6},{5,7},{6,4},{7,5},{8,10},{9,11},{10,... | collective-permute-start | bytes 884744 | tf_op jit(solution)/shard_map/ppermute | solution.py:107
  101.4 15.3 %collective-permute-start.20 = (bf16[144,2048]{1,0:T(8,128)(2,1)S(1)}, bf16[144,2048]{1,0:T(8,128)(2,1)S(1)}, u32[]{:S(2)}, u32[]{:S(2)}) collective-permute-start(bf16[144,2048]{1,0:T(8,128)(2,1)S(1)} %fusion.10), channel_id=1, source_target_pairs={{0,8},{1,9},{2,10},{3,11},{4,12},{5,13},{6,14},{7,15},{8,0},{9,1},... | collective-permute-start | bytes 1769480 | tf_op jit(solution)/shard_map/ppermute | solution.py:107
  108.4 15.2 %collective-permute-start.17 = (bf16[256,1024]{1,0:T(8,128)(2,1)}, bf16[256,1024]{1,0:T(8,128)(2,1)}, u32[]{:S(2)}, u32[]{:S(2)}) collective-permute-start(bf16[256,1024]{1,0:T(8,128)(2,1)} %pad_maximum_fusion.9.rest_2_), channel_id=1, source_target_pairs={{0,2},{1,3},{2,0},{3,1},{4,6},{5,7},{6,4},{7,5},{8,10},{9,11},{10,... | collective-permute-start | bytes 1572872 | tf_op jit(solution)/shard_map/ppermute | solution.py:107
  111.1 16.6 %collective-permute-start.15 = (bf16[288,1024]{1,0:T(8,128)(2,1)}, bf16[288,1024]{1,0:T(8,128)(2,1)}, u32[]{:S(2)}, u32[]{:S(2)}) collective-permute-start(bf16[288,1024]{1,0:T(8,128)(2,1)} %pad_maximum_fusion.rest_0_.rest_2_), channel_id=1, source_target_pairs={{0,4},{1,5},{2,6},{3,7},{4,0},{5,1},{6,2},{7,3},{8,12},{9,13},{10,... | collective-permute-start | bytes 1769480 | tf_op jit(solution)/shard_map/ppermute | solution.py:107
  117.4 14.0 %collective-permute-start.21 = (bf16[144,1024]{1,0:T(8,128)(2,1)}, bf16[144,1024]{1,0:T(8,128)(2,1)}, u32[]{:S(2)}, u32[]{:S(2)}) collective-permute-start(bf16[144,1024]{1,0:T(8,128)(2,1)} %slice.144), channel_id=1, source_target_pairs={{0,2},{1,3},{2,0},{3,1},{4,6},{5,7},{6,4},{7,5},{8,10},{9,11},{10,... | collective-permute-start | bytes 884744 | tf_op jit(solution)/shard_map/ppermute | solution.py:107
  118.9 14.6 %collective-permute-start.22 = (bf16[128,1024]{1,0:T(8,128)(2,1)}, bf16[128,1024]{1,0:T(8,128)(2,1)}, u32[]{:S(2)}, u32[]{:S(2)}) collective-permute-start(bf16[128,1024]{1,0:T(8,128)(2,1)} %slice.145), channel_id=1, source_target_pairs={{0,4},{1,5},{2,6},{3,7},{4,0},{5,1},{6,2},{7,3},{8,12},{9,13},{10,... | collective-permute-start | bytes 786440 | tf_op jit(solution)/shard_map/ppermute | solution.py:107
  123.6 26.8 %collective-permute-start.30 = (bf16[144,2048]{1,0:T(8,128)(2,1)}, bf16[144,2048]{1,0:T(8,128)(2,1)S(1)}, u32[]{:S(2)}, u32[]{:S(2)}) collective-permute-start(bf16[144,2048]{1,0:T(8,128)(2,1)} %copy-done.15), channel_id=1, source_target_pairs={{0,16},{1,17},{2,18},{3,19},{4,20},{5,21},{6,22},{7,23},{8,24},{9,... | collective-permute-start | bytes 1769480 | tf_op jit(solution)/shard_map/ppermute | solution.py:107
  131.3 22.3 %collective-permute-start.19 = (bf16[160,2048]{1,0:T(8,128)(2,1)S(1)}, bf16[160,2048]{1,0:T(8,128)(2,1)S(1)}, u32[]{:S(2)}, u32[]{:S(2)}) collective-permute-start(bf16[160,2048]{1,0:T(8,128)(2,1)S(1)} %get-tuple-element.50.rest_4_), channel_id=1, source_target_pairs={{0,1},{1,0},{2,3},{3,2},{4,5},{5,4},{6,7},{7,6},{8,9},{9,8},{10,11... | collective-permute-start | bytes 1966088 | tf_op jit(solution)/shard_map/ppermute | solution.py:107
  132.5 31.8 %collective-permute-start.23 = (bf16[288,1024]{1,0:T(8,128)(2,1)S(1)}, bf16[288,1024]{1,0:T(8,128)(2,1)S(1)}, u32[]{:S(2)}, u32[]{:S(2)}) collective-permute-start(bf16[288,1024]{1,0:T(8,128)(2,1)S(1)} %pad_maximum_fusion.1.rest_1_.rest_0_.rest_2_), channel_id=1, source_target_pairs={{0,4},{1,5},{2,6},{3,7},{4,0},{5,1},{6,2},{7,3},{8,12},{9,13},{10,... | collective-permute-start | bytes 1769480 | tf_op jit(solution)/shard_map/ppermute | solution.py:107
  134.5 29.8 %collective-permute-start.24 = (bf16[256,1024]{1,0:T(8,128)(2,1)S(1)}, bf16[256,1024]{1,0:T(8,128)(2,1)S(1)}, u32[]{:S(2)}, u32[]{:S(2)}) collective-permute-start(bf16[256,1024]{1,0:T(8,128)(2,1)S(1)} %pad_maximum_fusion.10.rest_2_), channel_id=1, source_target_pairs={{0,2},{1,3},{2,0},{3,1},{4,6},{5,7},{6,4},{7,5},{8,10},{9,11},{10,... | collective-permute-start | bytes 1572872 | tf_op jit(solution)/shard_map/ppermute | solution.py:107
  150.4 15.2 %collective-permute-start.35 = (bf16[144,2048]{1,0:T(8,128)(2,1)S(1)}, bf16[144,2048]{1,0:T(8,128)(2,1)S(1)}, u32[]{:S(2)}, u32[]{:S(2)}) collective-permute-start(bf16[144,2048]{1,0:T(8,128)(2,1)S(1)} %collective-permute-done.30), channel_id=1, source_target_pairs={{0,8},{1,9},{2,10},{3,11},{4,12},{5,13},{6,14},{7,15},{8,0},{9,1},... | collective-permute-start | bytes 1769480 | tf_op jit(solution)/shard_map/ppermute | solution.py:107
  165.5 8.4 %collective-permute-start.36 = (bf16[144,1024]{1,0:T(8,128)(2,1)S(1)}, bf16[144,1024]{1,0:T(8,128)(2,1)S(1)}, u32[]{:S(2)}, u32[]{:S(2)}) collective-permute-start(bf16[144,1024]{1,0:T(8,128)(2,1)S(1)} %slice.152), channel_id=1, source_target_pairs={{0,2},{1,3},{2,0},{3,1},{4,6},{5,7},{6,4},{7,5},{8,10},{9,11},{10,... | collective-permute-start | bytes 884744 | tf_op jit(solution)/shard_map/ppermute | solution.py:107
  165.8 9.2 %collective-permute-start.38 = (bf16[128,1024]{1,0:T(8,128)(2,1)S(1)}, bf16[128,1024]{1,0:T(8,128)(2,1)S(1)}, u32[]{:S(2)}, u32[]{:S(2)}) collective-permute-start(bf16[128,1024]{1,0:T(8,128)(2,1)S(1)} %slice.153), channel_id=1, source_target_pairs={{0,4},{1,5},{2,6},{3,7},{4,0},{5,1},{6,2},{7,3},{8,12},{9,13},{10,... | collective-permute-start | bytes 786440 | tf_op jit(solution)/shard_map/ppermute | solution.py:107
  174.0 17.5 %collective-permute-start.37 = (bf16[288,1024]{1,0:T(8,128)(2,1)S(1)}, bf16[288,1024]{1,0:T(8,128)(2,1)S(1)}, u32[]{:S(2)}, u32[]{:S(2)}) collective-permute-start(bf16[288,1024]{1,0:T(8,128)(2,1)S(1)} %pad_maximum_fusion.3.rest_1_.rest_0_.rest_2_), channel_id=1, source_target_pairs={{0,4},{1,5},{2,6},{3,7},{4,0},{5,1},{6,2},{7,3},{8,12},{9,13},{10,... | collective-permute-start | bytes 1769480 | tf_op jit(solution)/shard_map/ppermute | solution.py:107
  175.1 16.4 %collective-permute-start.39 = (bf16[256,1024]{1,0:T(8,128)(2,1)S(1)}, bf16[256,1024]{1,0:T(8,128)(2,1)S(1)}, u32[]{:S(2)}, u32[]{:S(2)}) collective-permute-start(bf16[256,1024]{1,0:T(8,128)(2,1)S(1)} %pad_maximum_fusion.12.rest_2_), channel_id=1, source_target_pairs={{0,2},{1,3},{2,0},{3,1},{4,6},{5,7},{6,4},{7,5},{8,10},{9,11},{10,... | collective-permute-start | bytes 1572872 | tf_op jit(solution)/shard_map/ppermute | solution.py:107
  176.9 24.2 %collective-permute-start.28 = (bf16[256,1024]{1,0:T(8,128)(2,1)S(1)}, bf16[256,1024]{1,0:T(8,128)(2,1)S(1)}, u32[]{:S(2)}, u32[]{:S(2)}) collective-permute-start(bf16[256,1024]{1,0:T(8,128)(2,1)S(1)} %get-tuple-element.58), channel_id=1, source_target_pairs={{0,2},{1,3},{2,0},{3,1},{4,6},{5,7},{6,4},{7,5},{8,10},{9,11},{10,... | collective-permute-start | bytes 1572872 | tf_op jit(solution)/shard_map/ppermute | solution.py:107
  177.2 24.2 %collective-permute-start.26 = (bf16[256,1024]{1,0:T(8,128)(2,1)S(1)}, bf16[256,1024]{1,0:T(8,128)(2,1)S(1)}, u32[]{:S(2)}, u32[]{:S(2)}) collective-permute-start(bf16[256,1024]{1,0:T(8,128)(2,1)S(1)} %get-tuple-element.56.rest_4_), channel_id=1, source_target_pairs={{0,4},{1,5},{2,6},{3,7},{4,0},{5,1},{6,2},{7,3},{8,12},{9,13},{10,... | collective-permute-start | bytes 1572872 | tf_op jit(solution)/shard_map/ppermute | solution.py:107
  191.5 10.1 %collective-permute-start.41 = (bf16[160,2048]{1,0:T(8,128)(2,1)S(1)}, bf16[160,2048]{1,0:T(8,128)(2,1)S(1)}, u32[]{:S(2)}, u32[]{:S(2)}) collective-permute-start(bf16[160,2048]{1,0:T(8,128)(2,1)S(1)} %get-tuple-element.63), channel_id=1, source_target_pairs={{0,1},{1,0},{2,3},{3,2},{4,5},{5,4},{6,7},{7,6},{8,9},{9,8},{10,11... | collective-permute-start | bytes 1966088 | tf_op jit(solution)/shard_map/ppermute | solution.py:107
  191.6 17.9 %collective-permute-start.31 = (bf16[144,1024]{1,0:T(8,128)(2,1)S(1)}, bf16[144,1024]{1,0:T(8,128)(2,1)S(1)}, u32[]{:S(2)}, u32[]{:S(2)}) collective-permute-start(bf16[144,1024]{1,0:T(8,128)(2,1)S(1)} %slice.150), channel_id=1, source_target_pairs={{0,2},{1,3},{2,0},{3,1},{4,6},{5,7},{6,4},{7,5},{8,10},{9,11},{10,... | collective-permute-start | bytes 884744 | tf_op jit(solution)/shard_map/ppermute | solution.py:107
  193.5 17.1 %collective-permute-start.33 = (bf16[128,1024]{1,0:T(8,128)(2,1)S(1)}, bf16[128,1024]{1,0:T(8,128)(2,1)S(1)}, u32[]{:S(2)}, u32[]{:S(2)}) collective-permute-start(bf16[128,1024]{1,0:T(8,128)(2,1)S(1)} %slice.151), channel_id=1, source_target_pairs={{0,4},{1,5},{2,6},{3,7},{4,0},{5,1},{6,2},{7,3},{8,12},{9,13},{10,... | collective-permute-start | bytes 786440 | tf_op jit(solution)/shard_map/ppermute | solution.py:107
  209.6 17.6 %collective-permute-start.32 = (bf16[288,1024]{1,0:T(8,128)(2,1)S(1)}, bf16[288,1024]{1,0:T(8,128)(2,1)S(1)}, u32[]{:S(2)}, u32[]{:S(2)}) collective-permute-start(bf16[288,1024]{1,0:T(8,128)(2,1)S(1)} %pad_maximum_fusion.2.rest_1_.rest_0_.rest_2_), channel_id=1, source_target_pairs={{0,4},{1,5},{2,6},{3,7},{4,0},{5,1},{6,2},{7,3},{8,12},{9,13},{10,... | collective-permute-start | bytes 1769480 | tf_op jit(solution)/shard_map/ppermute | solution.py:107
  210.7 16.5 %collective-permute-start.34 = (bf16[256,1024]{1,0:T(8,128)(2,1)S(1)}, bf16[256,1024]{1,0:T(8,128)(2,1)S(1)}, u32[]{:S(2)}, u32[]{:S(2)}) collective-permute-start(bf16[256,1024]{1,0:T(8,128)(2,1)S(1)} %pad_maximum_fusion.11.rest_2_), channel_id=1, source_target_pairs={{0,2},{1,3},{2,0},{3,1},{4,6},{5,7},{6,4},{7,5},{8,10},{9,11},{10,... | collective-permute-start | bytes 1572872 | tf_op jit(solution)/shard_map/ppermute | solution.py:107
  212.5 23.5 %collective-permute-start.45 = (bf16[256,1024]{1,0:T(8,128)(2,1)S(1)}, bf16[256,1024]{1,0:T(8,128)(2,1)S(1)}, u32[]{:S(2)}, u32[]{:S(2)}) collective-permute-start(bf16[256,1024]{1,0:T(8,128)(2,1)S(1)} %get-tuple-element.72), channel_id=1, source_target_pairs={{0,2},{1,3},{2,0},{3,1},{4,6},{5,7},{6,4},{7,5},{8,10},{9,11},{10,... | collective-permute-start | bytes 1572872 | tf_op jit(solution)/shard_map/ppermute | solution.py:107
  212.8 23.8 %collective-permute-start.44 = (bf16[256,1024]{1,0:T(8,128)(2,1)S(1)}, bf16[256,1024]{1,0:T(8,128)(2,1)S(1)}, u32[]{:S(2)}, u32[]{:S(2)}) collective-permute-start(bf16[256,1024]{1,0:T(8,128)(2,1)S(1)} %get-tuple-element.64.rest_4_), channel_id=1, source_target_pairs={{0,4},{1,5},{2,6},{3,7},{4,0},{5,1},{6,2},{7,3},{8,12},{9,13},{10,... | collective-permute-start | bytes 1572872 | tf_op jit(solution)/shard_map/ppermute | solution.py:107
  227.2 9.7 %collective-permute-start.43 = (bf16[160,2048]{1,0:T(8,128)(2,1)S(1)}, bf16[160,2048]{1,0:T(8,128)(2,1)S(1)}, u32[]{:S(2)}, u32[]{:S(2)}) collective-permute-start(bf16[160,2048]{1,0:T(8,128)(2,1)S(1)} %get-tuple-element.69), channel_id=1, source_target_pairs={{0,1},{1,0},{2,3},{3,2},{4,5},{5,4},{6,7},{7,6},{8,9},{9,8},{10,11... | collective-permute-start | bytes 1966088 | tf_op jit(solution)/shard_map/ppermute | solution.py:107
  244.5 15.1 %collective-permute-start.46 = (bf16[160,2048]{1,0:T(8,128)(2,1)S(1)}, bf16[160,2048]{1,0:T(8,128)(2,1)S(1)}, u32[]{:S(2)}, u32[]{:S(2)}) collective-permute-start(bf16[160,2048]{1,0:T(8,128)(2,1)S(1)} %get-tuple-element.75.rest_4_), channel_id=1, source_target_pairs={{0,1},{1,0},{2,3},{3,2},{4,5},{5,4},{6,7},{7,6},{8,9},{9,8},{10,11... | collective-permute-start | bytes 1966088 | tf_op jit(solution)/shard_map/ppermute | solution.py:107
  244.6 25.5 %collective-permute-start.49 = (bf16[256,1024]{1,0:T(8,128)(2,1)S(1)}, bf16[256,1024]{1,0:T(8,128)(2,1)S(1)}, u32[]{:S(2)}, u32[]{:S(2)}) collective-permute-start(bf16[256,1024]{1,0:T(8,128)(2,1)S(1)} %get-tuple-element.80), channel_id=1, source_target_pairs={{0,2},{1,3},{2,0},{3,1},{4,6},{5,7},{6,4},{7,5},{8,10},{9,11},{10,... | collective-permute-start | bytes 1572872 | tf_op jit(solution)/shard_map/ppermute | solution.py:107
  246.5 9.2 %collective-permute-start.59 = (bf16[128,1024]{1,0:T(8,128)(2,1)S(1)}, bf16[128,1024]{1,0:T(8,128)(2,1)S(1)}, u32[]{:S(2)}, u32[]{:S(2)}) collective-permute-start(bf16[128,1024]{1,0:T(8,128)(2,1)S(1)} %slice.210.rest_5_), channel_id=1, source_target_pairs={{0,4},{1,5},{2,6},{3,7},{4,0},{5,1},{6,2},{7,3},{8,12},{9,13},{10,... | collective-permute-start | bytes 786440 | tf_op jit(solution)/shard_map/ppermute | solution.py:107
  247.4 57.0 %collective-permute-start.29 = (bf16[128,1024]{1,0:T(8,128)(2,1)S(1)}, bf16[128,1024]{1,0:T(8,128)(2,1)S(1)}, u32[]{:S(2)}, u32[]{:S(2)}) collective-permute-start(bf16[128,1024]{1,0:T(8,128)(2,1)S(1)} %slice.212.rest_5_), channel_id=1, source_target_pairs={{0,4},{1,5},{2,6},{3,7},{4,0},{5,1},{6,2},{7,3},{8,12},{9,13},{10,... | collective-permute-start | bytes 786440 | tf_op jit(solution)/shard_map/ppermute | solution.py:107
  248.5 23.8 %collective-permute-start.58 = (bf16[128,1024]{1,0:T(8,128)(2,1)S(1)}, bf16[128,1024]{1,0:T(8,128)(2,1)S(1)}, u32[]{:S(2)}, u32[]{:S(2)}) collective-permute-start(bf16[128,1024]{1,0:T(8,128)(2,1)S(1)} %slice.211.rest_4_), channel_id=1, source_target_pairs={{0,2},{1,3},{2,0},{3,1},{4,6},{5,7},{6,4},{7,5},{8,10},{9,11},{10,... | collective-permute-start | bytes 786440 | tf_op jit(solution)/shard_map/ppermute | solution.py:107
  255.6 16.1 %collective-permute-start.48 = (bf16[256,1024]{1,0:T(8,128)(2,1)S(1)}, bf16[256,1024]{1,0:T(8,128)(2,1)S(1)}, u32[]{:S(2)}, u32[]{:S(2)}) collective-permute-start(bf16[256,1024]{1,0:T(8,128)(2,1)S(1)} %get-tuple-element.73.rest_4_), channel_id=1, source_target_pairs={{0,4},{1,5},{2,6},{3,7},{4,0},{5,1},{6,2},{7,3},{8,12},{9,13},{10,... | collective-permute-start | bytes 1572872 | tf_op jit(solution)/shard_map/ppermute | solution.py:107
  270.4 8.9 %collective-permute-start.55 = (bf16[128,1024]{1,0:T(8,128)(2,1)S(1)}, bf16[128,1024]{1,0:T(8,128)(2,1)S(1)}, u32[]{:S(2)}, u32[]{:S(2)}) collective-permute-start(bf16[128,1024]{1,0:T(8,128)(2,1)S(1)} %slice.208.rest_5_), channel_id=1, source_target_pairs={{0,4},{1,5},{2,6},{3,7},{4,0},{5,1},{6,2},{7,3},{8,12},{9,13},{10,... | collective-permute-start | bytes 786440 | tf_op jit(solution)/shard_map/ppermute | solution.py:107
  277.5 14.0 %collective-permute-start.52 = (bf16[256,1024]{1,0:T(8,128)(2,1)S(1)}, bf16[256,1024]{1,0:T(8,128)(2,1)S(1)}, u32[]{:S(2)}, u32[]{:S(2)}) collective-permute-start(bf16[256,1024]{1,0:T(8,128)(2,1)S(1)} %get-tuple-element.84), channel_id=1, source_target_pairs={{0,2},{1,3},{2,0},{3,1},{4,6},{5,7},{6,4},{7,5},{8,10},{9,11},{10,... | collective-permute-start | bytes 1572872 | tf_op jit(solution)/shard_map/ppermute | solution.py:107
  280.3 13.0 %collective-permute-start.50 = (bf16[256,1024]{1,0:T(8,128)(2,1)S(1)}, bf16[256,1024]{1,0:T(8,128)(2,1)S(1)}, u32[]{:S(2)}, u32[]{:S(2)}) collective-permute-start(bf16[256,1024]{1,0:T(8,128)(2,1)S(1)} %get-tuple-element.82), channel_id=1, source_target_pairs={{0,4},{1,5},{2,6},{3,7},{4,0},{5,1},{6,2},{7,3},{8,12},{9,13},{10,... | collective-permute-start | bytes 1572872 | tf_op jit(solution)/shard_map/ppermute | solution.py:107
  281.4 18.9 %collective-permute-start.56 = (bf16[128,2048]{1,0:T(8,128)(2,1)S(1)}, bf16[128,2048]{1,0:T(8,128)(2,1)S(1)}, u32[]{:S(2)}, u32[]{:S(2)}) collective-permute-start(bf16[128,2048]{1,0:T(8,128)(2,1)S(1)} %pad_maximum_fusion.13), channel_id=1, source_target_pairs={{0,8},{1,9},{2,10},{3,11},{4,12},{5,13},{6,14},{7,15},{8,0},{9,1},... | collective-permute-start | bytes 1572872 | tf_op jit(solution)/shard_map/ppermute | solution.py:107
  294.5 19.8 %collective-permute-start.60 = (bf16[128,2048]{1,0:T(8,128)(2,1)S(1)}, bf16[128,2048]{1,0:T(8,128)(2,1)S(1)}, u32[]{:S(2)}, u32[]{:S(2)}) collective-permute-start(bf16[128,2048]{1,0:T(8,128)(2,1)S(1)} %pad_maximum_fusion.14), channel_id=1, source_target_pairs={{0,8},{1,9},{2,10},{3,11},{4,12},{5,13},{6,14},{7,15},{8,0},{9,1},... | collective-permute-start | bytes 1572872 | tf_op jit(solution)/shard_map/ppermute | solution.py:107
  300.4 23.5 %collective-permute-start.57 = (bf16[128,2048]{1,0:T(8,128)(2,1)S(1)}, bf16[128,2048]{1,0:T(8,128)(2,1)S(1)}, u32[]{:S(2)}, u32[]{:S(2)}) collective-permute-start(bf16[128,2048]{1,0:T(8,128)(2,1)S(1)} %fusion.7), channel_id=1, source_target_pairs={{0,16},{1,17},{2,18},{3,19},{4,20},{5,21},{6,22},{7,23},{8,24},{9,... | collective-permute-start | bytes 1572872 | tf_op jit(solution)/shard_map/ppermute | solution.py:107
  (38 other events, 429.5 us)
